TPU v7x, 32 devices: a whole 2x2x4 slice. The times are simulated.
32 devices in a mesh: dp: 8 (over z, core), tp: 4 (over y, x).
Axes of the slice: x: 2, y: 2, z: 4, core: 2. Of those that a mesh axis runs over, the one named last changes fastest.
Arguments:
- tokens: bfloat16 [1024, 2048], P(('dp', 'tp')), may hold values from -6 to 6
- norm_gain: float32 [2048], replicated, may hold values from 0.5 to 1.5
- w_query: bfloat16 [2048, 2048], P('dp', 'tp'), may hold values from -0.125 to 0.125
- w_key: bfloat16 [2048, 2048], P('dp', 'tp'), may hold values from -0.125 to 0.125
- w_value: bfloat16 [2048, 4096], P('dp', 'tp'), may hold values from -0.125 to 0.125
- w_gate: bfloat16 [2048, 4096], P('dp', 'tp'), may hold values from -0.125 to 0.125
- w_beta: bfloat16 [2048, 32], P('dp', 'tp'), may hold values from -0.125 to 0.125
- w_decay: bfloat16 [2048, 32], P('dp', 'tp'), may hold values from -0.125 to 0.125
- conv_query: float32 [4, 2048], P(None, 'tp'), may hold values from -3 to 3
- conv_key: float32 [4, 2048], P(None, 'tp'), may hold values from -3 to 3
- conv_value: float32 [4, 4096], P(None, 'tp'), may hold values from -3 to 3
- decay_rate: float32 [32], P('tp'), may hold values from 0.004 to 0.04
- dt_bias: float32 [32], P('tp'), may hold values from -1 to 1
- out_gain: float32 [128], replicated, may hold values from 0.5 to 1.5
- seg_ids: int32 [8, 128], P('dp'), may hold values from 0 to 15, never falling along the last dimension, each value on 1 to 32 neighbouring positions
Outputs:
- mixed_tiles: bfloat16 [1024, 4096], P(('dp', 'tp'))
Inputs may be any that keep to these rules, and one draw needn't show every extreme that they name: Each row of seg_ids never falls; every prompt covers 1 to 32 consecutive positions.
All inputs are finite; a program needn't handle non-finite values.
Results may differ from a plain program's by a relative error of at most 0.0034.
The roundings to bfloat16 on the way count: a program that leaves them out, or rounds other values in their place, can miss the bound.
Values may be sent and summed in bfloat16 or wider, within the bound.
A program may use at most 64 MiB of HBM per device.

v0:
```python
import jax
import jax.numpy as jnp
from jax import lax
from jax.sharding import PartitionSpec as P

DK = 128
DV = 128
SPAN = 64


highest = lax.Precision.HIGHEST


def rms_rows(tokens, gain):
    floats = tokens.astype(jnp.float32)
    scaled = floats * lax.rsqrt(jnp.mean(floats * floats, axis=-1, keepdims=True) + 1e-06)
    return (scaled * gain).astype(jnp.bfloat16)


def split_columns(projected, column_counts):
    pieces = []
    offset = 0
    for count in column_counts:
        pieces.append(projected[:, offset : offset + count])
        offset = offset + count
    return pieces


def causal_conv(projected, kernel, segment):
    kernel_len = kernel.shape[0]
    summed = projected * kernel[kernel_len - 1]
    for offset in range(1, kernel_len):
        zeros_top = jnp.zeros((offset, projected.shape[1]), jnp.float32)
        shifted = jnp.concatenate([zeros_top, projected[:-offset]], axis=0)
        earlier = jnp.concatenate([jnp.full((offset,), -1, jnp.int32), segment[:-offset]])
        same_doc = (earlier == segment).astype(jnp.float32)
        summed = summed + shifted * same_doc[:, None] * kernel[kernel_len - 1 - offset]
    return jax.nn.silu(summed)


def unit_heads(values, heads, head_size):
    shaped = values.reshape(values.shape[0], heads, head_size)
    return shaped * lax.rsqrt(jnp.sum(shaped * shaped, axis=-1, keepdims=True) + 1e-06)


def delta_head(query, key_rows, value, beta, log_decay, segment):
    row_count = query.shape[0]
    blocks = row_count // SPAN
    value_size = value.shape[1]
    q_blocks = query.reshape(blocks, SPAN, query.shape[1])
    k_blocks = key_rows.reshape(blocks, SPAN, key_rows.shape[1])
    v_blocks = value.reshape(blocks, SPAN, value_size)
    beta_blocks = beta.reshape(blocks, SPAN)
    decay_blocks = log_decay.reshape(blocks, SPAN)
    seg_blocks = segment.reshape(blocks, SPAN)
    before = jnp.concatenate([jnp.full((1,), -1, jnp.int32), seg_blocks[:-1, -1]])
    row_index = lax.broadcasted_iota(jnp.int32, (SPAN, SPAN), 0)
    col_index = lax.broadcasted_iota(jnp.int32, (SPAN, SPAN), 1)
    lower_mask = row_index >= col_index
    strict = row_index > col_index

    def advance(state, inputs):
        block_q, block_k, block_v, block_beta, block_decay, block_seg, block_before = inputs
        cumulative = jnp.cumsum(block_decay)
        same_doc = block_seg[:, None] == block_seg[None, :]
        spread = jnp.where(lower_mask, cumulative[:, None] - cumulative[None, :], 0.0)
        decay_matrix = jnp.where(lower_mask & same_doc, jnp.exp(spread), 0.0)
        carried = (block_seg == block_before).astype(jnp.float32)
        from_start = jnp.exp(cumulative) * carried
        key_gram = jnp.dot(block_k, block_k.T, precision=highest)
        lower_matrix = jnp.where(strict, block_beta[:, None] * key_gram * decay_matrix, 0.0)
        system = jnp.eye(SPAN, dtype=jnp.float32) + lower_matrix
        right_side = jnp.concatenate(
            [block_beta[:, None] * block_v, (block_beta * from_start)[:, None] * block_k], axis=1
        )
        solved = lax.linalg.triangular_solve(
            system, right_side, left_side=True, lower=True, unit_diagonal=True
        )
        updates = solved[:, :value_size] - jnp.dot(solved[:, value_size:], state, precision=highest)
        scores = jnp.dot(block_q, block_k.T, precision=highest) * decay_matrix
        output = jnp.dot(from_start[:, None] * block_q, state, precision=highest) + jnp.dot(
            scores, updates, precision=highest
        )
        tail_weight = jnp.where(
            block_seg == block_seg[-1], jnp.exp(cumulative[-1] - cumulative), 0.0
        )
        new_state = jnp.exp(cumulative[-1]) * carried[-1] * state + jnp.dot(
            (tail_weight[:, None] * block_k).T, updates, precision=highest
        )
        return (new_state, output)

    initial = jnp.zeros((key_rows.shape[1], value_size), jnp.float32)
    last_state, outputs = lax.scan(
        advance,
        initial,
        (q_blocks, k_blocks, v_blocks, beta_blocks, decay_blocks, seg_blocks, before),
    )
    return outputs.reshape(row_count, value_size)


def prepare_heads(parts, segment, conv_query, conv_key, conv_value, decay_rate, dt_bias):
    proj_query, proj_key, proj_value, proj_gate, proj_beta, proj_decay = [
        piece_part.astype(jnp.float32) for piece_part in parts
    ]
    key_heads = proj_query.shape[1] // DK
    value_heads = proj_value.shape[1] // DV
    repeat = value_heads // key_heads
    query = unit_heads(causal_conv(proj_query, conv_query, segment), key_heads, DK) * DK ** (-0.5)
    keys = unit_heads(causal_conv(proj_key, conv_key, segment), key_heads, DK)
    values = causal_conv(proj_value, conv_value, segment).reshape(
        proj_value.shape[0], value_heads, DV
    )
    query = jnp.repeat(query, repeat, axis=1)
    keys = jnp.repeat(keys, repeat, axis=1)
    beta = jax.nn.sigmoid(proj_beta)
    log_decay = -decay_rate * jax.nn.softplus(proj_decay + dt_bias)
    gate_act = jax.nn.silu(proj_gate.reshape(proj_gate.shape[0], value_heads, DV))
    return (query, keys, values, beta, log_decay, gate_act)


def finish_heads(mixed, gate_act, out_gain):
    normed = mixed * lax.rsqrt(jnp.mean(mixed * mixed, axis=-1, keepdims=True) + 1e-06) * out_gain
    return (normed * gate_act).astype(jnp.bfloat16)


def shards(
    tokens,
    norm_gain,
    w_query,
    w_key,
    w_value,
    w_gate,
    w_beta,
    w_decay,
    conv_query,
    conv_key,
    conv_value,
    decay_rate,
    dt_bias,
    out_gain,
    seg_ids,
):
    gathered = (
        lax.all_gather(w_query, "dp", axis=0, tiled=True),
        lax.all_gather(w_key, "dp", axis=0, tiled=True),
        lax.all_gather(w_value, "dp", axis=0, tiled=True),
        lax.all_gather(w_gate, "dp", axis=0, tiled=True),
        lax.all_gather(w_beta, "dp", axis=0, tiled=True),
        lax.all_gather(w_decay, "dp", axis=0, tiled=True),
    )
    column_counts = [matrix.shape[1] for matrix in gathered]
    joined = jnp.concatenate(gathered, axis=1)
    projected = jnp.dot(
        rms_rows(lax.all_gather(tokens, "tp", axis=0, tiled=True), norm_gain),
        joined,
        preferred_element_type=jnp.float32,
    ).astype(jnp.bfloat16)
    parts = split_columns(projected, column_counts)
    segment = seg_ids[0]
    query, keys, values, beta, log_decay, gate_act = prepare_heads(
        parts, segment, conv_query, conv_key, conv_value, decay_rate, dt_bias
    )
    row_count = values.shape[0]
    local_heads = values.shape[1]
    mixed = jax.vmap(delta_head, in_axes=(1, 1, 1, 1, 1, None), out_axes=1)(
        query, keys, values, beta, log_decay, segment
    )
    tiles = finish_heads(mixed, gate_act, out_gain).reshape(row_count, local_heads * DV)
    return lax.all_to_all(tiles, "tp", split_axis=0, concat_axis=1, tiled=True)


def solution(mesh):
    in_specs = (
        P(("dp", "tp"), None),
        P(),
        P("dp", "tp"),
        P("dp", "tp"),
        P("dp", "tp"),
        P("dp", "tp"),
        P("dp", "tp"),
        P("dp", "tp"),
        P(None, "tp"),
        P(None, "tp"),
        P(None, "tp"),
        P("tp"),
        P("tp"),
        P(),
        P("dp", None),
    )
    out_specs = P(("dp", "tp"), None)
    return jax.shard_map(shards, mesh=mesh, in_specs=in_specs, out_specs=out_specs, check_vma=False)
```

profile of v0, /device:TPU:0, one launch (start us, length us, event | category | flops | bytes accessed | tf_op | source)
XLA Modules:
  0.0 318.1 jit_solution(6046680718237279407)
XLA Ops:
  6.5 0.7 all-gather.5.cloned.1.call-update
  7.3 0.7 all-gather.7.cloned.1.call-update
  8.1 0.7 all-gather.9.cloned.1.call-update
  9.8 1.3 reduce.5
  11.8 0.7 neg.25
  12.5 15.9 %all_gather.27 = bf16[2048,8]{0,1:T(8,128)(2,1)S(1)} all-gather(bf16[256,8]{0,1:T(8,128)(2,1)} %param.24), channel_id=1, replica_groups=mesh['dp'=8,'tp'=4] {'dp'}, dimensions={0}, use_global_device_ids=true | all-gather | bytes 36864 | tf_op jit(solution)/shard_map/all_gather | solution.py:149
  28.7 14.3 %all_gather.26 = bf16[2048,8]{0,1:T(8,128)(2,1)S(1)} all-gather(bf16[256,8]{0,1:T(8,128)(2,1)} %param.23), channel_id=1, replica_groups=mesh['dp'=8,'tp'=4] {'dp'}, dimensions={0}, use_global_device_ids=true | all-gather | bytes 36864 | tf_op jit(solution)/shard_map/all_gather | solution.py:148
  43.2 11.1 %all_gather.21 = bf16[128,2048]{1,0:T(8,128)(2,1)S(1)} all-gather(bf16[32,2048]{1,0:T(8,128)(2,1)} %param.17), channel_id=1, replica_groups=mesh['dp'=8,'tp'=4] {'tp'}, dimensions={0}, use_global_device_ids=true | all-gather | bytes 655360 | tf_op jit(solution)/shard_map/all_gather | solution.py:154
  54.3 0.7 pad_add_fusion
  55.2 0.7 slice_bitcast_fusion.2
  57.2 0.7 compare_convert_fusion.3
  57.9 0.9 fusion.60
  58.8 0.9 fusion.61
  59.6 0.9 fusion.59
  60.6 10.8 %all-gather.7.cloned.1.call-done = bf16[2048,512]{1,0:T(8,128)(2,1)} async-done(((bf16[256,512]{1,0:T(8,128)(2,1)}), bf16[2048,512]{1,0:T(8,128)(2,1)}) %all-gather.7.cloned.1.call-update) | async-done | bytes 2097168 | tf_op jit(solution)/shard_map/all_gather | solution.py:145
  71.4 48.3 %all-gather.9.cloned.1.call-done = bf16[2048,1024]{1,0:T(8,128)(2,1)} async-done(((bf16[256,1024]{1,0:T(8,128)(2,1)}), bf16[2048,1024]{1,0:T(8,128)(2,1)}) %all-gather.9.cloned.1.call-update) | async-done | bytes 4194320 | tf_op jit(solution)/shard_map/all_gather | solution.py:146
  119.7 47.4 %all-gather.11.cloned.1.call-done = bf16[2048,1024]{1,0:T(8,128)(2,1)} async-done(((bf16[256,1024]{1,0:T(8,128)(2,1)}), bf16[2048,1024]{1,0:T(8,128)(2,1)}) %all-gather.11.cloned.1.call-update) | async-done | bytes 4194320 | tf_op jit(solution)/shard_map/all_gather | solution.py:147
  167.0 18.8 %concatenate.57 = bf16[2048,3088]{1,0:T(8,128)(2,1)} concatenate(bf16[2048,512]{1,0:T(8,128)(2,1)} %all-gather.5.cloned.1.call-done, bf16[2048,512]{1,0:T(8,128)(2,1)} %all-gather.7.cloned.1.call-done, bf16[2048,1024]{1,0:T(8,128)(2,1)} %all-gather.9.cloned.1.call-done, bf16[2048,1024]{1,0:T(8,128)(2,1)} %all-gather.11.cloned.1.call-done, bf16[2048,8]{1,0:T(8,128)(2,1)S(1)} %copy.40, ...), dimensions={1} | concatenate | bytes 25296896 | tf_op jit(solution)/shard_map/concatenate | solution.py:152
  185.8 8.3 %convolution_convert_fusion = bf16[128,3088]{0,1:T(8,128)(2,1)S(1)} fusion(bf16[2048,3088]{1,0:T(8,128)(2,1)} %concatenate.57, bf16[128,2048]{1,0:T(8,128)(2,1)S(1)} %all_gather.21, f32[2048]{0:T(1024)S(1)} %copy-done, f32[128]{0:T(128)S(1)} %add_rsqrt_fusion.3), kind=kOutput, calls=%fused_computation.70 | convolution fusion | flops 1620445184 | bytes 13971968 | tf_op jit(solution)/shard_map/dot_general | solution.py:153
  194.5 1.2 multiply_reduce_fusion
  195.9 0.8 copy.43
  196.8 1.2 divide_multiply_fusion
  198.2 1.0 broadcast_in_dim.35
  199.2 101.2 %while.14 = (s32[]{:T(128)}, f32[8,128,128]{2,1,0:T(8,128)S(1)}, f32[2,8,64,128]{3,2,0,1:T(8,128)S(1)}, f32[2,8,64]{2,1,0:T(8,128)S(1)}, s32[2,64]{1,0:T(2,128)S...) while((s32[]{:T(128)}, f32[8,128,128]{2,1,0:T(8,128)S(1)}, ...), condition=%wide.region_5.6_spmd.clone.clone, body=%wide.region_3.5_spmd.clone.clone.sunk | while | flops 555329344 | bytes 8479040 | solution.py:93
  204.2 1.3 fusion.98
  205.6 40.0 %custom-call.8 = f32[8,1,64,64]{2,3,1,0:T(8,128)S(1)} custom-call(f32[8,1,64,64]{3,2,1,0:T(8,128)} %fusion.98), custom_call_target="InvertDiagBlocksLowerTriangular" | custom-call | tf_op jit(solution)/shard_map/vmap()/while/body/eval_jaxpr/triangular_solve | solution.py:76
  248.7 1.1 convolution_add_fusion.3
  254.8 1.3 fusion.98
  256.1 40.0 %custom-call.8 = f32[8,1,64,64]{2,3,1,0:T(8,128)S(1)} custom-call(f32[8,1,64,64]{3,2,1,0:T(8,128)} %fusion.98), custom_call_target="InvertDiagBlocksLowerTriangular" | custom-call | tf_op jit(solution)/shard_map/vmap()/while/body/eval_jaxpr/triangular_solve | solution.py:76
  299.3 1.1 convolution_add_fusion.3
  301.3 9.6 %all_to_all.19 = bf16[4,32,1024]{2,1,0:T(8,128)(2,1)S(1)} all-to-all(bf16[4,32,1024]{2,1,0:T(8,128)(2,1)S(1)} %all_to_all.14), channel_id=1, replica_groups=mesh['dp'=8,'tp'=4] {'tp'}, dimensions={0} | all-to-all | bytes 524288 | tf_op jit(solution)/shard_map/all_to_all | solution.py:169
  310.9 0.7 copy.74
  (83 shorter events, 20.4 us)
Async XLA Ops:
  6.5 54.0 %all-gather.5.cloned.1.call-start = ((), (), s32[]{:S(2)}) async-start(), calls=%async_computation.1 | async-start | bytes 2359296 | tf_op jit(solution)/shard_map/all_gather | solution.py:144
  7.3 64.1 %all-gather.7.cloned.1.call-start = ((), (), s32[]{:S(2)}) async-start(), calls=%async_computation.2 | async-start | bytes 2359296 | tf_op jit(solution)/shard_map/all_gather | solution.py:145
  8.0 111.6 %all-gather.9.cloned.1.call-start = ((), (), s32[]{:S(2)}) async-start(), calls=%async_computation.3 | async-start | bytes 4718592 | tf_op jit(solution)/shard_map/all_gather | solution.py:146
  8.7 158.3 %all-gather.11.cloned.1.call-start = ((), (), s32[]{:S(2)}) async-start(), calls=%async_computation.4 | async-start | bytes 4718592 | tf_op jit(solution)/shard_map/all_gather | solution.py:147
  60.5 125.3 %copy-start = (f32[2048]{0:T(1024)S(1)}, f32[2048]{0:T(1024)}, u32[]{:S(2)}) copy-start(f32[2048]{0:T(1024)} %param.18) | copy-start | bytes 24580
  185.8 8.4 %copy-start.2 = (f32[8]{0:T(128)S(1)}, f32[8]{0:T(128)}, u32[]{:S(2)}) copy-start(f32[8]{0:T(128)} %param.29) | copy-start | bytes 100
  199.2 101.6 %copy-start.1 = (f32[128]{0:T(128)S(1)}, f32[128]{0:T(128)}, u32[]{:S(2)}) copy-start(f32[128]{0:T(128)} %param.30) | copy-start | bytes 1540
Sparse Core Ops, SparseCore 0:
  9.0 32.0 all-gather.4
  42.7 28.6 all-gather.6
  73.0 46.6 all-gather.8
  121.1 45.8 all-gather.10
where the time goes:
time: 319 us; the launch traced here: 318 us
  waiting for transfers between devices  109 us (34%)
  other arithmetic  92 us (29%)
  blocking collectives  50.8 us (16%)
  local copies, waits for them, and re-layouts  32.7 us (10%)
  matrix products  18.8 us (6%)
  between operations  13.4 us (4%)
    another operation x8, other arithmetic, advance(): lax.linalg.triangular_solve(system, right_side, left_side=True, lower=Tru...  80.4 us
    all_gather x1, waiting for transfers between devices, shards(): lax.all_gather(w_value, 'dp', axis=0, tiled=True)  48.3 us
    all_gather x1, waiting for transfers between devices, shards(): lax.all_gather(w_gate, 'dp', axis=0, tiled=True)  47.4 us
    concatenate x1, local copies, waits for them, and re-layouts, shards(): joined = jnp.concatenate(gathered, axis=1)  18.8 us
    all_gather x1, blocking collectives, shards(): lax.all_gather(w_decay, 'dp', axis=0, tiled=True)  15.9 us
    all_gather x1, blocking collectives, shards(): lax.all_gather(w_beta, 'dp', axis=0, tiled=True)  14.3 us
    all_gather x1, blocking collectives, shards(): lax.all_gather(tokens, 'tp', axis=0, tiled=True)  11.1 us
    all_gather x1, waiting for transfers between devices, shards(): lax.all_gather(w_key, 'dp', axis=0, tiled=True)  10.8 us
  transfers between devices with their start and end apart: 4, of which 3 were waited for; matrix products, arithmetic and copies ran while one was open for 3% of the time, Pallas kernels for 0%

commit v1 on v0

--- a/solution.py
+++ b/solution.py
@@ -1,6 +1,10 @@
+import functools
+
 import jax
 import jax.numpy as jnp
 from jax import lax
+from jax.experimental import pallas as pl
+from jax.experimental.pallas import tpu as pltpu
 from jax.sharding import PartitionSpec as P
 
 DK = 128
@@ -169,6 +173,409 @@
     return lax.all_to_all(tiles, "tp", split_axis=0, concat_axis=1, tiled=True)
 
 
+MESH = pl.DeviceIdType.MESH
+CORES = 2
+STEP = 8
+
+
+def dot_exact(left, right):
+    return jnp.dot(left, right, precision=highest, preferred_element_type=jnp.float32)
+
+
+def dot_rows(left, right, precision=None):
+    return lax.dot_general(
+        left,
+        right,
+        (((1,), (1,)), ((), ())),
+        precision=precision,
+        preferred_element_type=jnp.float32,
+    )
+
+
+def sigmoid(x):
+    return 1.0 / (1.0 + jnp.exp(-x))
+
+
+def unit_rows(values):
+    return values * lax.rsqrt(jnp.sum(values * values, axis=-1, keepdims=True) + 1e-06)
+
+
+def conv_rows(projected, taps, same_before):
+    summed = projected * taps[3:4]
+    for offset in range(1, 4):
+        shifted = pltpu.roll(projected, offset, 0)
+        mask = same_before[offset - 1]
+        if projected.shape[1] > mask.shape[1]:
+            mask = jnp.concatenate([mask] * (projected.shape[1] // mask.shape[1]), axis=1)
+        summed = summed + jnp.where(mask, shifted, 0.0) * taps[3 - offset : 4 - offset]
+    return summed * sigmoid(summed)
+
+
+def mix_groups(z, nz, heads, tok, weights, ba, seg, taps_q, taps_k, taps_v, rate, bias, gain, out):
+    rows = seg.shape[2]
+    row = lax.broadcasted_iota(jnp.int32, (rows, rows), 0)
+    col = lax.broadcasted_iota(jnp.int32, (rows, rows), 1)
+    lower = row >= col
+    strict = row > col
+    eye = jnp.where(row == col, 1.0, 0.0)
+    ones_lower = jnp.where(lower, 1.0, 0.0)
+    width = heads * DV
+    count = rate.shape[1]
+    lane = lax.broadcasted_iota(jnp.int32, (rows, count), 1)
+    tq = taps_q[:, pl.ds(pl.multiple_of(z * DK, DK), DK)]
+    tk = taps_k[:, pl.ds(pl.multiple_of(z * DK, DK), DK)]
+    tv = taps_v[:, pl.ds(pl.multiple_of(z * width, width), width)]
+    sources, depth = weights.shape[0], weights.shape[1]
+
+    def block(size):
+        return row // size == col // size
+
+    chains = []
+    gates = []
+    for g in range(nz):
+        rows_g = tok[g].reshape(rows, tok.shape[3])
+        full = weights[...].reshape(sources * depth, weights.shape[2])
+        projected = jnp.dot(rows_g, full, preferred_element_type=jnp.float32)
+        projected = projected.astype(jnp.bfloat16).astype(jnp.float32)
+        small = jnp.zeros((rows, ba.shape[1]), jnp.float32)
+        for s in range(sources):
+            small = small + dot_rows(rows_g[:, s * depth : (s + 1) * depth], ba[s])
+        small = small.astype(jnp.bfloat16).astype(jnp.float32)
+        beta_all = sigmoid(small[:, :count])
+        shifted = small[:, count : 2 * count] + bias[...]
+        soft = jnp.maximum(shifted, 0.0) + jnp.log1p(jnp.exp(-jnp.abs(shifted)))
+        cumulative = dot_exact(ones_lower, -rate[...] * soft)
+        seg_row = jnp.broadcast_to(seg[g][0:1].astype(jnp.float32), (rows, rows))
+        seg_col = seg_row.T
+        same = seg_row == seg_col
+        same_before = [
+            (pltpu.roll(seg_col, offset, 0) == seg_col) & (row >= offset) for offset in range(1, 4)
+        ]
+        query = unit_rows(conv_rows(projected[:, :DK], tq, same_before)) * DK ** (-0.5)
+        key = unit_rows(conv_rows(projected[:, DK : 2 * DK], tk, same_before))
+        values = conv_rows(projected[:, 2 * DK : 2 * DK + width], tv, same_before)
+        gate = projected[:, 2 * DK + width :]
+        key_gram = dot_rows(key, key, highest)
+        query_gram = dot_rows(query, key, highest)
+        gates.append(gate * sigmoid(gate))
+        for h in range(heads):
+            pick = lane == z * heads + h
+            beta = jnp.sum(jnp.where(pick, beta_all, 0.0), axis=1, keepdims=True)
+            total = jnp.sum(jnp.where(pick, cumulative, 0.0), axis=1, keepdims=True)
+            total = jnp.broadcast_to(total, (rows, rows))
+            spread = jnp.where(lower, total - total.T, 0.0)
+            decay = jnp.where(lower & same, jnp.exp(spread), 0.0)
+            chains.append(
+                (
+                    jnp.where(strict, beta * key_gram * decay, 0.0),
+                    query_gram * decay,
+                    beta * values[:, h * DV : (h + 1) * DV],
+                )
+            )
+    lows = [c[0] for c in chains]
+    inner = [jnp.where(block(STEP), m, 0.0) for m in lows]
+    squares = [dot_exact(m, m) for m in inner]
+    fourths = [dot_exact(m, m) for m in squares]
+    firsts = [eye - m + s - dot_exact(m, s) for m, s in zip(inner, squares)]
+    inverse = [f + dot_exact(f, q) for f, q in zip(firsts, fourths)]
+    size = STEP
+    while size < rows // 4:
+        ring = block(2 * size) & jnp.logical_not(block(size))
+        parts = [dot_exact(jnp.where(ring, m, 0.0), t) for m, t in zip(lows, inverse)]
+        inverse = [t - dot_exact(t, p) for t, p in zip(inverse, parts)]
+        size = 2 * size
+    outer = jnp.logical_not(block(size))
+    solved = [dot_exact(t, c[2]) for t, c in zip(inverse, chains)]
+    parts = [dot_exact(jnp.where(outer, m, 0.0), x) for m, x in zip(lows, solved)]
+    solved = [x - dot_exact(t, p) for x, t, p in zip(solved, inverse, parts)]
+    mixed = [dot_exact(c[1], x) for c, x in zip(chains, solved)]
+    for g in range(nz):
+        for h in range(heads):
+            m = mixed[g * heads + h]
+            normed = m * lax.rsqrt(jnp.mean(m * m, axis=-1, keepdims=True) + 1e-06) * gain[...]
+            tile = (normed * gates[g][:, h * DV : (h + 1) * DV]).astype(jnp.bfloat16)
+            for t in range(out.shape[1]):
+                share = rows // out.shape[1]
+                out[g, t, :, h * DV : (h + 1) * DV] = tile[t * share : (t + 1) * share]
+
+
+def layer_kernel(
+    nz,
+    ntp,
+    heads,
+    tokens,
+    norm_gain,
+    w_query,
+    w_key,
+    w_value,
+    w_gate,
+    w_ba,
+    taps_q,
+    taps_k,
+    taps_v,
+    rate,
+    bias,
+    gain,
+    seg_own,
+    out,
+    tok,
+    weights,
+    ba,
+    seg,
+    tiles,
+    zs,
+    zr,
+    ys,
+    yr,
+    ws,
+    wr,
+    os,
+    orr,
+    rs,
+    rr,
+    bs,
+    br,
+    brs,
+    brr,
+    ss,
+    sr,
+    cs,
+    cr,
+    local,
+):
+    dp = lax.axis_index("dp")
+    tp = lax.axis_index("tp")
+    z = dp // CORES
+    core = dp % CORES
+    sibling = (z * CORES + 1 - core, tp)
+    width = heads * DV
+
+    def z_at(k):
+        return lax.rem(z + k, nz)
+
+    def dp_at(k):
+        return z_at(k) * CORES + core
+
+    def tp_at(j):
+        return lax.rem(tp + j, ntp)
+
+    def remote(source, target, send, recv, device):
+        return pltpu.make_async_remote_copy(
+            src_ref=source,
+            dst_ref=target,
+            send_sem=send,
+            recv_sem=recv,
+            device_id=device,
+            device_id_type=MESH,
+        )
+
+    barrier = pltpu.get_barrier_semaphore()
+    for k in range(nz):
+        for j in range(ntp):
+            if k or j:
+                pl.semaphore_signal(
+                    barrier, inc=1, device_id=(dp_at(k), tp_at(j)), device_id_type=MESH
+                )
+    pl.semaphore_signal(barrier, inc=1, device_id=sibling, device_id_type=MESH)
+
+    floats = tokens[...].astype(jnp.float32)
+    scaled = floats * lax.rsqrt(jnp.mean(floats * floats, axis=-1, keepdims=True) + 1e-06)
+    tok[z, tp] = (scaled * norm_gain[...]).astype(jnp.bfloat16)
+    seg[z] = seg_own[...]
+    ba[dp] = w_ba[...]
+
+    def pieces(chip):
+        return (
+            (w_query.at[:, pl.ds(pl.multiple_of(chip * DK, DK), DK)], 0, DK),
+            (w_key.at[:, pl.ds(pl.multiple_of(chip * DK, DK), DK)], DK, DK),
+            (w_value.at[:, pl.ds(pl.multiple_of(chip * width, width), width)], 2 * DK, width),
+            (w_gate.at[:, pl.ds(pl.multiple_of(chip * width, width), width)], 2 * DK + width, width),
+        )
+
+    own_local = []
+    for i, (source, start, size) in enumerate(pieces(z)):
+        copy = pltpu.make_async_copy(source, weights.at[dp, :, pl.ds(start, size)], local.at[i])
+        copy.start()
+        own_local.append(copy)
+
+    pl.semaphore_wait(barrier, nz * ntp)
+
+    sends = []
+    tok_z = []
+    seg_z = []
+    ba_z = []
+    for k in range(1, nz):
+        peer = (dp_at(k), tp)
+        copy = remote(tok.at[z, tp], tok.at[z, tp], zs.at[k], zr.at[k], peer)
+        copy.start()
+        tok_z.append(copy)
+        copy = remote(seg.at[z], seg.at[z], ss.at[k], sr.at[k], peer)
+        copy.start()
+        seg_z.append(copy)
+        copy = remote(ba.at[dp], ba.at[dp], bs.at[k], br.at[k], peer)
+        copy.start()
+        ba_z.append(copy)
+    tok_y = []
+
+    def spread_rows(k):
+        at = lax.rem(z + nz - k, nz)
+        for j in range(1, ntp):
+            copy = remote(
+                tok.at[at, tp], tok.at[at, tp], ys.at[k, j], yr.at[k, j], (dp, tp_at(j))
+            )
+            copy.start()
+            tok_y.append(copy)
+
+    spread_rows(0)
+    weight_z = []
+    for k in range(1, nz):
+        for i, (source, start, size) in enumerate(pieces(z_at(k))):
+            copy = remote(
+                source,
+                weights.at[dp, :, pl.ds(start, size)],
+                ws.at[k, i],
+                wr.at[k, i],
+                (dp_at(k), tp),
+            )
+            copy.start()
+            weight_z.append(copy)
+    own_sibling = []
+    for i, (source, start, size) in enumerate(pieces(z)):
+        copy = remote(
+            source, weights.at[dp, :, pl.ds(start, size)], os.at[i], orr.at[i], sibling
+        )
+        copy.start()
+        own_sibling.append(copy)
+    ba_own = remote(ba.at[dp], ba.at[dp], brs.at[0], brr.at[0], sibling)
+    ba_own.start()
+
+    for k in range(1, nz):
+        tok_z[k - 1].wait_recv()
+        spread_rows(k)
+    relays = []
+    for k in range(1, nz):
+        at = lax.rem(z + nz - k, nz) * CORES + core
+        ba_z[k - 1].wait_recv()
+        copy = remote(ba.at[at], ba.at[at], brs.at[k], brr.at[k], sibling)
+        copy.start()
+        relays.append(copy)
+        for i in range(4):
+            weight_z[(k - 1) * 4 + i].wait_recv()
+        copy = remote(weights.at[at], weights.at[at], rs.at[k], rr.at[k], sibling)
+        copy.start()
+        relays.append(copy)
+    for copy in own_local:
+        copy.wait()
+    for copy in tok_z + ba_z + weight_z:
+        copy.wait_send()
+    for copy in seg_z + tok_y + own_sibling + relays + [ba_own]:
+        copy.wait()
+
+    mix_groups(
+        z, nz, heads, tok, weights, ba, seg, taps_q, taps_k, taps_v, rate, bias, gain, tiles
+    )
+
+    place = pl.ds(pl.multiple_of((tp * nz + z) * width, width), width)
+    finals = []
+    for k in range(nz):
+        for j in range(ntp):
+            source = tiles.at[z_at(k), tp_at(j)]
+            if k or j:
+                copy = remote(
+                    source, out.at[:, place], cs.at[k, j], cr.at[k, j], (dp_at(k), tp_at(j))
+                )
+            else:
+                copy = pltpu.make_async_copy(source, out.at[:, place], cs.at[0, 0])
+            copy.start()
+            finals.append(copy)
+    for copy in finals:
+        copy.wait()
+
+
+def layer(n_dp, n_tp, *args):
+    (
+        tokens,
+        norm_gain,
+        w_query,
+        w_key,
+        w_value,
+        w_gate,
+        w_beta,
+        w_decay,
+        conv_query,
+        conv_key,
+        conv_value,
+        decay_rate,
+        dt_bias,
+        out_gain,
+        seg_ids,
+    ) = args
+    nz = n_dp // CORES
+    rows = seg_ids.shape[1]
+    share, model = tokens.shape
+    depth = w_query.shape[0]
+    value_heads = w_value.shape[1] // DV
+    if n_dp % CORES or w_query.shape[1] // DK != nz or value_heads % nz or rows != 128:
+        return shards(*args)
+    heads = value_heads // nz
+    wide = 2 * DK + 2 * heads * DV
+    w_ba = jnp.concatenate([w_beta, w_decay], axis=1).T
+    small = w_ba.shape[0]
+    vmem = pl.BlockSpec(memory_space=pltpu.VMEM)
+    anywhere = pl.BlockSpec(memory_space=pl.ANY)
+    dma = pltpu.SemaphoreType.DMA
+    return pl.pallas_call(
+        functools.partial(layer_kernel, nz, n_tp, heads),
+        out_shape=jax.ShapeDtypeStruct((share, n_tp * value_heads * DV), jnp.bfloat16),
+        in_specs=[vmem, vmem] + [anywhere] * 4 + [vmem] * 8,
+        out_specs=vmem,
+        scratch_shapes=[
+            pltpu.VMEM((nz, n_tp, share, model), jnp.bfloat16),
+            pltpu.VMEM((n_dp, depth, wide), jnp.bfloat16),
+            pltpu.VMEM((n_dp, small, depth), jnp.bfloat16),
+            pltpu.VMEM((nz, 8, rows), jnp.int32),
+            pltpu.VMEM((nz, n_tp, share, heads * DV), jnp.bfloat16),
+            dma((nz,)),
+            dma((nz,)),
+            dma((nz, n_tp)),
+            dma((nz, n_tp)),
+            dma((nz, 4)),
+            dma((nz, 4)),
+            dma((4,)),
+            dma((4,)),
+            dma((nz,)),
+            dma((nz,)),
+            dma((nz,)),
+            dma((nz,)),
+            dma((nz,)),
+            dma((nz,)),
+            dma((nz,)),
+            dma((nz,)),
+            dma((nz, n_tp)),
+            dma((nz, n_tp)),
+            dma((4,)),
+        ],
+        compiler_params=pltpu.CompilerParams(
+            collective_id=0, has_side_effects=True, vmem_limit_bytes=48 * 2**20
+        ),
+    )(
+        tokens,
+        norm_gain.reshape(1, -1),
+        w_query,
+        w_key,
+        w_value,
+        w_gate,
+        w_ba,
+        conv_query,
+        conv_key,
+        conv_value,
+        decay_rate.reshape(1, -1),
+        dt_bias.reshape(1, -1),
+        out_gain.reshape(1, -1),
+        jnp.broadcast_to(seg_ids, (8, rows)),
+    )
+
+
 def solution(mesh):
     in_specs = (
         P(("dp", "tp"), None),
@@ -188,4 +595,5 @@
         P("dp", None),
     )
     out_specs = P(("dp", "tp"), None)
-    return jax.shard_map(shards, mesh=mesh, in_specs=in_specs, out_specs=out_specs, check_vma=False)
+    body = functools.partial(layer, mesh.shape["dp"], mesh.shape["tp"])
+    return jax.shard_map(body, mesh=mesh, in_specs=in_specs, out_specs=out_specs, check_vma=False)

time: 319 us -> 82.4 us (0.26)
  waiting for transfers between devices: 109 us -> 0 us
  other arithmetic: 92 us -> 0.76 us
  Pallas kernels: 0 us -> 73.5 us
  blocking collectives: 50.8 us -> 0 us
  local copies, waits for them, and re-layouts: 32.7 us -> 7.67 us
  matrix products: 18.8 us -> 0 us
  between operations: 13.4 us -> 0.05 us
    all_gather x4 -> x0, waiting for transfers between devices: 106 us -> none  [the longest x1 48.3 us: shards(): lax.all_gather(w_value, 'dp', axis=0, tiled=True)]
    another operation x10 -> x0, other arithmetic: 80.9 us -> none  [the longest x8 80.4 us: advance(): lax.linalg.triangular_solve(system, right_side, left_side=True, lower=Tru...]
    pallas_call x0 -> x1, Pallas kernels: none -> 73.5 us  [layer(): pl.pallas_call(functools.partial(layer_kernel, nz, n_tp, heads), out_shap...]
    all_gather x3 -> x0, blocking collectives: 41.2 us -> none  [the longest x1 15.9 us: shards(): lax.all_gather(w_decay, 'dp', axis=0, tiled=True)]
    concatenate x2 -> x0, local copies, waits for them, and re-layouts: 19.5 us -> none  [the longest x1 18.8 us: shards(): joined = jnp.concatenate(gathered, axis=1)]
    dot_general x13 -> x0, matrix products: 17.5 us -> none  [the longest x1 8.32 us: shards(): jnp.dot(rms_rows(lax.all_gather(tokens, 'tp', axis=0, tiled=True), norm_g...]
    all_to_all x1 -> x0, blocking collectives: 9.57 us -> none  [shards(): return lax.all_to_all(tiles, 'tp', split_axis=0, concat_axis=1, tiled=True)]
    slice x12 -> x0, local copies, waits for them, and re-layouts: 7.33 us -> none  [the longest x3 2.6 us: causal_conv(): summed = projected * kernel[kernel_len - 1]]
  transfers between devices with their start and end apart: 4 -> 0, of which waited for: 3 -> 0; matrix products, arithmetic and copies ran while one was open for 3% -> 0% of each run, Pallas kernels for 0% -> 0%
where the time goes in v1:
time: 82.4 us; the launch traced here: 82 us
  Pallas kernels  73.5 us (89%)
  local copies, waits for them, and re-layouts  7.67 us (9%)
    pallas_call x1, Pallas kernels, layer(): pl.pallas_call(functools.partial(layer_kernel, nz, n_tp, heads), out_shap...  73.5 us
    unnamed x25, local copies, waits for them, and re-layouts  7 us

profile of v1, /device:TPU:0, one launch (start us, length us, event | category | flops | bytes accessed | tf_op | source)
XLA Modules:
  0.0 82.0 jit_solution(9482393203812633041)
XLA Ops:
  0.0 0.0 copy-start.5
  0.0 0.7 broadcast_in_dim.8.seg_own
  0.7 0.0 copy-start.6
  0.7 0.0 copy-start.9
  0.7 0.0 copy-start.10
  0.7 0.0 copy-start.11
  0.7 0.8 maximum_bitcast_fusion.w_ba
  1.4 0.0 copy-done.5
  1.4 0.0 copy-done.6
  1.4 0.0 copy-done.9
  1.5 0.0 copy-done.10
  1.5 0.0 copy-done.11
  1.5 0.0 copy-start
  1.5 1.0 %copy-done = bf16[256,1024]{1,0:T(8,128)(2,1)S(1)} copy-done((bf16[256,1024]{1,0:T(8,128)(2,1)S(1)}, bf16[256,1024]{1,0:T(8,128)(2,1)}, u32[]{:S(2)}) %copy-start) | copy-done | bytes 524312
  2.5 0.0 copy-start.1
  2.5 1.0 %copy-done.1 = bf16[256,1024]{1,0:T(8,128)(2,1)S(1)} copy-done((bf16[256,1024]{1,0:T(8,128)(2,1)S(1)}, bf16[256,1024]{1,0:T(8,128)(2,1)}, u32[]{:S(2)}) %copy-start.1) | copy-done | bytes 524312
  3.6 0.0 copy-start.2
  3.6 0.9 %copy-done.2 = bf16[256,512]{1,0:T(8,128)(2,1)S(1)} copy-done((bf16[256,512]{1,0:T(8,128)(2,1)S(1)}, bf16[256,512]{1,0:T(8,128)(2,1)}, u32[]{:S(2)}) %copy-start.2) | copy-done | bytes 262168
  4.5 0.0 copy-start.3
  4.5 0.9 %copy-done.3 = bf16[256,512]{1,0:T(8,128)(2,1)S(1)} copy-done((bf16[256,512]{1,0:T(8,128)(2,1)S(1)}, bf16[256,512]{1,0:T(8,128)(2,1)}, u32[]{:S(2)}) %copy-start.3) | copy-done | bytes 262168
  5.5 0.0 copy-start.4
  5.5 0.9 %copy-done.4 = bf16[32,2048]{1,0:T(8,128)(2,1)S(1)} copy-done((bf16[32,2048]{1,0:T(8,128)(2,1)S(1)}, bf16[32,2048]{1,0:T(8,128)(2,1)}, u32[]{:S(2)}) %copy-start.4) | copy-done | bytes 131096
  6.4 0.0 copy-start.7
  6.4 0.7 copy-done.7
  7.1 0.0 copy-start.8
  7.1 0.7 copy-done.8
  7.8 73.5 %shard_map.145 = bf16[32,4096]{1,0:T(8,128)(2,1)S(1)} custom-call(bf16[32,2048]{1,0:T(8,128)(2,1)S(1)} %copy-done.4, f32[1,2048]{1,0:T(1,128)S(1)} %bitcast.7, bf16[256,512]{1,0:T(8,128)(2,1)S(1)} %copy-done.2, bf16[256,512]{1,0:T(8,128)(2,1)S(1)} %copy-done.3, bf16[256,1024]{1,0:T(8,128)(2,1)S(1)} %copy-done, bf16[256,1024]{1,0:T(8,128)(2,1)S(1)} %copy-done.1, ...), custom_call_target="tpu_custom_call" | custom-call | tf_op jit(solution)/shard_map/pallas_call | solution.py:527
  81.3 0.7 copy.17
Async XLA Ops:
  0.0 1.4 %copy-start.5 = (f32[4,1024]{1,0:T(4,128)S(1)}, f32[4,1024]{1,0:T(4,128)}, u32[]{:S(2)}) copy-start(f32[4,1024]{1,0:T(4,128)} %taps_v.1) | copy-start | bytes 49156
  0.7 0.8 copy-start.6
  0.7 0.8 copy-start.9
  0.7 0.8 copy-start.10
  0.7 0.8 copy-start.11
  1.5 1.0 %copy-start = (bf16[256,1024]{1,0:T(8,128)(2,1)S(1)}, bf16[256,1024]{1,0:T(8,128)(2,1)}, u32[]{:S(2)}) copy-start(bf16[256,1024]{1,0:T(8,128)(2,1)} %w_value.1) | copy-start | bytes 1572868
  2.5 1.0 %copy-start.1 = (bf16[256,1024]{1,0:T(8,128)(2,1)S(1)}, bf16[256,1024]{1,0:T(8,128)(2,1)}, u32[]{:S(2)}) copy-start(bf16[256,1024]{1,0:T(8,128)(2,1)} %w_gate.1) | copy-start | bytes 1572868
  3.6 0.9 %copy-start.2 = (bf16[256,512]{1,0:T(8,128)(2,1)S(1)}, bf16[256,512]{1,0:T(8,128)(2,1)}, u32[]{:S(2)}) copy-start(bf16[256,512]{1,0:T(8,128)(2,1)} %w_query.1) | copy-start | bytes 786436
  4.5 0.9 %copy-start.3 = (bf16[256,512]{1,0:T(8,128)(2,1)S(1)}, bf16[256,512]{1,0:T(8,128)(2,1)}, u32[]{:S(2)}) copy-start(bf16[256,512]{1,0:T(8,128)(2,1)} %w_key.1) | copy-start | bytes 786436
  5.5 0.9 %copy-start.4 = (bf16[32,2048]{1,0:T(8,128)(2,1)S(1)}, bf16[32,2048]{1,0:T(8,128)(2,1)}, u32[]{:S(2)}) copy-start(bf16[32,2048]{1,0:T(8,128)(2,1)} %tokens.1) | copy-start | bytes 393220
  6.4 0.7 copy-start.7
  7.1 0.7 copy-start.8

commit v2 on v1

--- a/solution.py
+++ b/solution.py
@@ -211,68 +211,12 @@
     return summed * sigmoid(summed)
 
 
-def mix_groups(z, nz, heads, tok, weights, ba, seg, taps_q, taps_k, taps_v, rate, bias, gain, out):
-    rows = seg.shape[2]
-    row = lax.broadcasted_iota(jnp.int32, (rows, rows), 0)
-    col = lax.broadcasted_iota(jnp.int32, (rows, rows), 1)
-    lower = row >= col
-    strict = row > col
+def inverse_blocks(lows, row, col, rows):
     eye = jnp.where(row == col, 1.0, 0.0)
-    ones_lower = jnp.where(lower, 1.0, 0.0)
-    width = heads * DV
-    count = rate.shape[1]
-    lane = lax.broadcasted_iota(jnp.int32, (rows, count), 1)
-    tq = taps_q[:, pl.ds(pl.multiple_of(z * DK, DK), DK)]
-    tk = taps_k[:, pl.ds(pl.multiple_of(z * DK, DK), DK)]
-    tv = taps_v[:, pl.ds(pl.multiple_of(z * width, width), width)]
-    sources, depth = weights.shape[0], weights.shape[1]
 
     def block(size):
         return row // size == col // size
 
-    chains = []
-    gates = []
-    for g in range(nz):
-        rows_g = tok[g].reshape(rows, tok.shape[3])
-        full = weights[...].reshape(sources * depth, weights.shape[2])
-        projected = jnp.dot(rows_g, full, preferred_element_type=jnp.float32)
-        projected = projected.astype(jnp.bfloat16).astype(jnp.float32)
-        small = jnp.zeros((rows, ba.shape[1]), jnp.float32)
-        for s in range(sources):
-            small = small + dot_rows(rows_g[:, s * depth : (s + 1) * depth], ba[s])
-        small = small.astype(jnp.bfloat16).astype(jnp.float32)
-        beta_all = sigmoid(small[:, :count])
-        shifted = small[:, count : 2 * count] + bias[...]
-        soft = jnp.maximum(shifted, 0.0) + jnp.log1p(jnp.exp(-jnp.abs(shifted)))
-        cumulative = dot_exact(ones_lower, -rate[...] * soft)
-        seg_row = jnp.broadcast_to(seg[g][0:1].astype(jnp.float32), (rows, rows))
-        seg_col = seg_row.T
-        same = seg_row == seg_col
-        same_before = [
-            (pltpu.roll(seg_col, offset, 0) == seg_col) & (row >= offset) for offset in range(1, 4)
-        ]
-        query = unit_rows(conv_rows(projected[:, :DK], tq, same_before)) * DK ** (-0.5)
-        key = unit_rows(conv_rows(projected[:, DK : 2 * DK], tk, same_before))
-        values = conv_rows(projected[:, 2 * DK : 2 * DK + width], tv, same_before)
-        gate = projected[:, 2 * DK + width :]
-        key_gram = dot_rows(key, key, highest)
-        query_gram = dot_rows(query, key, highest)
-        gates.append(gate * sigmoid(gate))
-        for h in range(heads):
-            pick = lane == z * heads + h
-            beta = jnp.sum(jnp.where(pick, beta_all, 0.0), axis=1, keepdims=True)
-            total = jnp.sum(jnp.where(pick, cumulative, 0.0), axis=1, keepdims=True)
-            total = jnp.broadcast_to(total, (rows, rows))
-            spread = jnp.where(lower, total - total.T, 0.0)
-            decay = jnp.where(lower & same, jnp.exp(spread), 0.0)
-            chains.append(
-                (
-                    jnp.where(strict, beta * key_gram * decay, 0.0),
-                    query_gram * decay,
-                    beta * values[:, h * DV : (h + 1) * DV],
-                )
-            )
-    lows = [c[0] for c in chains]
     inner = [jnp.where(block(STEP), m, 0.0) for m in lows]
     squares = [dot_exact(m, m) for m in inner]
     fourths = [dot_exact(m, m) for m in squares]
@@ -285,46 +229,51 @@
         inverse = [t - dot_exact(t, p) for t, p in zip(inverse, parts)]
         size = 2 * size
     outer = jnp.logical_not(block(size))
-    solved = [dot_exact(t, c[2]) for t, c in zip(inverse, chains)]
-    parts = [dot_exact(jnp.where(outer, m, 0.0), x) for m, x in zip(lows, solved)]
-    solved = [x - dot_exact(t, p) for x, t, p in zip(solved, inverse, parts)]
-    mixed = [dot_exact(c[1], x) for c, x in zip(chains, solved)]
-    for g in range(nz):
-        for h in range(heads):
-            m = mixed[g * heads + h]
-            normed = m * lax.rsqrt(jnp.mean(m * m, axis=-1, keepdims=True) + 1e-06) * gain[...]
-            tile = (normed * gates[g][:, h * DV : (h + 1) * DV]).astype(jnp.bfloat16)
-            for t in range(out.shape[1]):
-                share = rows // out.shape[1]
-                out[g, t, :, h * DV : (h + 1) * DV] = tile[t * share : (t + 1) * share]
+    return inverse, [jnp.where(outer, m, 0.0) for m in lows]
 
 
 def layer_kernel(
     nz,
     ntp,
     heads,
-    tokens,
-    norm_gain,
+    tokens_hbm,
+    gain_hbm,
     w_query,
     w_key,
     w_value,
     w_gate,
-    w_ba,
+    beta_hbm,
+    decay_hbm,
+    taps_q_hbm,
+    taps_k_hbm,
+    taps_v_hbm,
+    rate_hbm,
+    bias_hbm,
+    out_gain_hbm,
+    seg_hbm,
+    out,
+    tokens,
+    norm_gain,
+    w_beta,
+    w_decay,
     taps_q,
     taps_k,
     taps_v,
     rate,
     bias,
-    gain,
-    seg_own,
-    out,
+    out_gain,
     tok,
-    weights,
+    w_first,
+    w_second,
+    w_third,
     ba,
     seg,
     tiles,
+    loads,
     zs,
     zr,
+    fs,
+    fr,
     ys,
     yr,
     ws,
@@ -353,6 +302,9 @@
     def z_at(k):
         return lax.rem(z + k, nz)
 
+    def z_from(k):
+        return lax.rem(z + nz - k, nz)
+
     def dp_at(k):
         return z_at(k) * CORES + core
 
@@ -360,7 +312,7 @@
         return lax.rem(tp + j, ntp)
 
     def remote(source, target, send, recv, device):
-        return pltpu.make_async_remote_copy(
+        copy = pltpu.make_async_remote_copy(
             src_ref=source,
             dst_ref=target,
             send_sem=send,
@@ -368,6 +320,29 @@
             device_id=device,
             device_id_type=MESH,
         )
+        copy.start()
+        return copy
+
+    def load(i, source, target):
+        copy = pltpu.make_async_copy(source, target, loads.at[i])
+        copy.start()
+        return copy
+
+    early = [
+        load(0, tokens_hbm, tokens),
+        load(1, gain_hbm, norm_gain),
+        load(2, beta_hbm, w_beta),
+        load(3, decay_hbm, w_decay),
+        load(4, seg_hbm, seg.at[z]),
+    ]
+    later = [
+        load(5, taps_q_hbm, taps_q),
+        load(6, taps_k_hbm, taps_k),
+        load(7, taps_v_hbm, taps_v),
+        load(8, rate_hbm, rate),
+        load(9, bias_hbm, bias),
+        load(10, out_gain_hbm, out_gain),
+    ]
 
     barrier = pltpu.get_barrier_semaphore()
     for k in range(nz):
@@ -378,116 +353,238 @@
                 )
     pl.semaphore_signal(barrier, inc=1, device_id=sibling, device_id_type=MESH)
 
+    def columns(chip, size):
+        return pl.ds(pl.multiple_of(chip * size, size), size)
+
+    def pieces(chip):
+        return (
+            (w_query.at[:, columns(chip, DK)], w_first.at[dp, :, 0:DK]),
+            (w_key.at[:, columns(chip, DK)], w_first.at[dp, :, DK : 2 * DK]),
+            (w_value.at[:, columns(chip, width)], w_second.at[dp]),
+            (w_gate.at[:, columns(chip, width)], w_third.at[dp]),
+        )
+
+    for copy in early:
+        copy.wait()
+    own_local = []
+    for i, (source, target) in enumerate(pieces(z)):
+        copy = pltpu.make_async_copy(source, target, local.at[i])
+        copy.start()
+        own_local.append(copy)
+
     floats = tokens[...].astype(jnp.float32)
     scaled = floats * lax.rsqrt(jnp.mean(floats * floats, axis=-1, keepdims=True) + 1e-06)
     tok[z, tp] = (scaled * norm_gain[...]).astype(jnp.bfloat16)
-    seg[z] = seg_own[...]
-    ba[dp] = w_ba[...]
-
-    def pieces(chip):
-        return (
-            (w_query.at[:, pl.ds(pl.multiple_of(chip * DK, DK), DK)], 0, DK),
-            (w_key.at[:, pl.ds(pl.multiple_of(chip * DK, DK), DK)], DK, DK),
-            (w_value.at[:, pl.ds(pl.multiple_of(chip * width, width), width)], 2 * DK, width),
-            (w_gate.at[:, pl.ds(pl.multiple_of(chip * width, width), width)], 2 * DK + width, width),
-        )
-
-    own_local = []
-    for i, (source, start, size) in enumerate(pieces(z)):
-        copy = pltpu.make_async_copy(source, weights.at[dp, :, pl.ds(start, size)], local.at[i])
-        copy.start()
-        own_local.append(copy)
+    count = w_beta.shape[1]
+    pick_row = lax.broadcasted_iota(jnp.int32, (2 * count, count), 0)
+    pick_col = lax.broadcasted_iota(jnp.int32, (2 * count, count), 1)
+    pick_beta = jnp.where(pick_row == pick_col, 1.0, 0.0).astype(jnp.bfloat16)
+    pick_decay = jnp.where(pick_row == pick_col + count, 1.0, 0.0).astype(jnp.bfloat16)
+    ba[dp] = (dot_rows(pick_beta, w_beta[...]) + dot_rows(pick_decay, w_decay[...])).astype(
+        jnp.bfloat16
+    )
 
     pl.semaphore_wait(barrier, nz * ntp)
 
-    sends = []
-    tok_z = []
+    half = nz // 2
+    near = [k for k in range(1, half)]
+    far = half
+    mirror = z + half - 2 * half * (z // half)
+
+    def in_half(k):
+        return (z // half) * half + lax.rem(z + k, half)
+
+    def in_half_from(k):
+        return (z // half) * half + lax.rem(z + half - k, half)
+
+    def other(chip):
+        return lax.rem(chip + half, nz)
+
+    def device_of(chip):
+        return (chip * CORES + core, tp)
+
+    tok_far = remote(
+        tok.at[z, tp], tok.at[z, tp], zs.at[far], zr.at[far], device_of(mirror)
+    )
+    tok_near = [
+        remote(tok.at[z, tp], tok.at[z, tp], zs.at[k], zr.at[k], device_of(in_half(k)))
+        for k in near
+    ]
     seg_z = []
     ba_z = []
     for k in range(1, nz):
         peer = (dp_at(k), tp)
-        copy = remote(tok.at[z, tp], tok.at[z, tp], zs.at[k], zr.at[k], peer)
-        copy.start()
-        tok_z.append(copy)
-        copy = remote(seg.at[z], seg.at[z], ss.at[k], sr.at[k], peer)
-        copy.start()
-        seg_z.append(copy)
-        copy = remote(ba.at[dp], ba.at[dp], bs.at[k], br.at[k], peer)
-        copy.start()
-        ba_z.append(copy)
-    tok_y = []
-
-    def spread_rows(k):
-        at = lax.rem(z + nz - k, nz)
-        for j in range(1, ntp):
-            copy = remote(
-                tok.at[at, tp], tok.at[at, tp], ys.at[k, j], yr.at[k, j], (dp, tp_at(j))
+        seg_z.append(remote(seg.at[z], seg.at[z], ss.at[k], sr.at[k], peer))
+        ba_z.append(remote(ba.at[dp], ba.at[dp], bs.at[k], br.at[k], peer))
+
+    def spread_rows(n, at):
+        return [
+            remote(tok.at[at, tp], tok.at[at, tp], ys.at[n, j], yr.at[n, j], (dp, tp_at(j)))
+            for j in range(1, ntp)
+        ]
+
+    tok_y = spread_rows(0, z)
+    farthest = [nz // 2] + [k for k in range(1, nz) if k != nz // 2]
+    weight_z = {}
+    for i in range(4):
+        for k in farthest:
+            source, target = pieces(z_at(k))[i]
+            weight_z[i, k] = remote(source, target, ws.at[k, i], wr.at[k, i], (dp_at(k), tp))
+        if i == 1:
+            tok_far.wait_recv()
+            tok_pass = [
+                remote(
+                    tok.at[mirror, tp],
+                    tok.at[mirror, tp],
+                    fs.at[k],
+                    fr.at[k],
+                    device_of(in_half(k)),
+                )
+                for k in near
+            ]
+            tok_y += spread_rows(1, mirror)
+    own_sibling = []
+    for i, (source, target) in enumerate(pieces(z)):
+        own_sibling.append(remote(source, target, os.at[i], orr.at[i], sibling))
+    ba_own = remote(ba.at[dp], ba.at[dp], brs.at[0], brr.at[0], sibling)
+
+    slot = 2
+    for k in near:
+        tok_near[k - 1].wait_recv()
+        tok_y += spread_rows(slot, in_half_from(k))
+        tok_pass[k - 1].wait_recv()
+        tok_y += spread_rows(slot + 1, other(in_half_from(k)))
+        slot += 2
+
+    relays = []
+
+    def relay(stage, which, ref):
+        passed = []
+        for k in farthest:
+            at = z_from(k) * CORES + core
+            for i in which:
+                weight_z[i, k].wait_recv()
+            passed.append(
+                remote(ref.at[at], ref.at[at], rs.at[stage, k], rr.at[stage, k], sibling)
             )
-            copy.start()
-            tok_y.append(copy)
-
-    spread_rows(0)
-    weight_z = []
+        for i in which:
+            own_local[i].wait()
+            own_sibling[i].wait_recv()
+        for copy in passed:
+            copy.wait_recv()
+        relays.extend(passed)
+
     for k in range(1, nz):
-        for i, (source, start, size) in enumerate(pieces(z_at(k))):
-            copy = remote(
-                source,
-                weights.at[dp, :, pl.ds(start, size)],
-                ws.at[k, i],
-                wr.at[k, i],
-                (dp_at(k), tp),
-            )
-            copy.start()
-            weight_z.append(copy)
-    own_sibling = []
-    for i, (source, start, size) in enumerate(pieces(z)):
-        copy = remote(
-            source, weights.at[dp, :, pl.ds(start, size)], os.at[i], orr.at[i], sibling
-        )
-        copy.start()
-        own_sibling.append(copy)
-    ba_own = remote(ba.at[dp], ba.at[dp], brs.at[0], brr.at[0], sibling)
-    ba_own.start()
-
-    for k in range(1, nz):
-        tok_z[k - 1].wait_recv()
-        spread_rows(k)
-    relays = []
-    for k in range(1, nz):
-        at = lax.rem(z + nz - k, nz) * CORES + core
+        at = z_from(k) * CORES + core
         ba_z[k - 1].wait_recv()
-        copy = remote(ba.at[at], ba.at[at], brs.at[k], brr.at[k], sibling)
-        copy.start()
-        relays.append(copy)
-        for i in range(4):
-            weight_z[(k - 1) * 4 + i].wait_recv()
-        copy = remote(weights.at[at], weights.at[at], rs.at[k], rr.at[k], sibling)
-        copy.start()
-        relays.append(copy)
-    for copy in own_local:
+        relays.append(remote(ba.at[at], ba.at[at], brs.at[k], brr.at[k], sibling))
+    ba_own.wait_recv()
+    for copy in list(relays):
+        copy.wait_recv()
+    for copy in seg_z + tok_y:
+        copy.wait_recv()
+    for copy in later:
         copy.wait()
-    for copy in tok_z + ba_z + weight_z:
-        copy.wait_send()
-    for copy in seg_z + tok_y + own_sibling + relays + [ba_own]:
-        copy.wait()
-
-    mix_groups(
-        z, nz, heads, tok, weights, ba, seg, taps_q, taps_k, taps_v, rate, bias, gain, tiles
-    )
-
-    place = pl.ds(pl.multiple_of((tp * nz + z) * width, width), width)
+    relay(0, (0, 1), w_first)
+
+    rows = seg.shape[2]
+    sources, depth = ba.shape[0], ba.shape[2]
+    model = tok.shape[3]
+    row = lax.broadcasted_iota(jnp.int32, (rows, rows), 0)
+    col = lax.broadcasted_iota(jnp.int32, (rows, rows), 1)
+    lower = row >= col
+    strict = row > col
+    ones_lower = jnp.where(lower, 1.0, 0.0)
+    lane = lax.broadcasted_iota(jnp.int32, (rows, count), 1)
+
+    def project(chip, ref):
+        left = tok[chip].reshape(rows, model)
+        right = ref[...].reshape(sources * depth, ref.shape[2])
+        result = jnp.dot(left, right, preferred_element_type=jnp.float32)
+        return result.astype(jnp.bfloat16).astype(jnp.float32)
+
+    order = [z_at(k) for k in farthest] + [z]
+    tq = taps_q[:, columns(z, DK)]
+    tk = taps_k[:, columns(z, DK)]
+    tv = taps_v[:, columns(z, width)]
+    lows, scores, betas, befores = [], [], [], []
+    for chip in order:
+        projected = project(chip, w_first)
+        left = tok[chip].reshape(rows, model)
+        small = jnp.zeros((rows, 2 * count), jnp.float32)
+        for s in range(sources):
+            small = small + dot_rows(left[:, s * depth : (s + 1) * depth], ba[s])
+        small = small.astype(jnp.bfloat16).astype(jnp.float32)
+        beta_all = sigmoid(small[:, :count])
+        shifted = small[:, count:] + bias[...]
+        soft = jnp.maximum(shifted, 0.0) + jnp.log1p(jnp.exp(-jnp.abs(shifted)))
+        cumulative = dot_exact(ones_lower, -rate[...] * soft)
+        seg_row = jnp.broadcast_to(seg[chip].astype(jnp.float32), (rows, rows))
+        seg_col = seg_row.T
+        same = seg_row == seg_col
+        same_before = [
+            (pltpu.roll(seg_col, offset, 0) == seg_col) & (row >= offset) for offset in range(1, 4)
+        ]
+        query = unit_rows(conv_rows(projected[:, :DK], tq, same_before)) * DK ** (-0.5)
+        key = unit_rows(conv_rows(projected[:, DK:], tk, same_before))
+        key_gram = dot_rows(key, key, highest)
+        query_gram = dot_rows(query, key, highest)
+        befores.append(same_before)
+        for h in range(heads):
+            pick = lane == z * heads + h
+            beta = jnp.sum(jnp.where(pick, beta_all, 0.0), axis=1, keepdims=True)
+            total = jnp.sum(jnp.where(pick, cumulative, 0.0), axis=1, keepdims=True)
+            total = jnp.broadcast_to(total, (rows, rows))
+            spread = jnp.where(lower, total - total.T, 0.0)
+            decay = jnp.where(lower & same, jnp.exp(spread), 0.0)
+            betas.append(beta)
+            lows.append(jnp.where(strict, beta * key_gram * decay, 0.0))
+            scores.append(query_gram * decay)
+    inverse, outer = inverse_blocks(lows, row, col, rows)
+
+    relay(1, (2,), w_second)
+    rights = []
+    for n, chip in enumerate(order):
+        values = conv_rows(project(chip, w_second), tv, befores[n])
+        for h in range(heads):
+            rights.append(betas[n * heads + h] * values[:, h * DV : (h + 1) * DV])
+    solved = [dot_exact(t, b) for t, b in zip(inverse, rights)]
+    parts = [dot_exact(m, x) for m, x in zip(outer, solved)]
+    solved = [x - dot_exact(t, p) for x, t, p in zip(solved, inverse, parts)]
+    mixed = [dot_exact(s, x) for s, x in zip(scores, solved)]
+    normed = [
+        m * lax.rsqrt(jnp.mean(m * m, axis=-1, keepdims=True) + 1e-06) * out_gain[...]
+        for m in mixed
+    ]
+
+    relay(2, (3,), w_third)
+    place = columns(tp * nz + z, width)
+    share = rows // ntp
     finals = []
-    for k in range(nz):
+    for n, chip in enumerate(order):
+        gate = project(chip, w_third)
+        gate = gate * sigmoid(gate)
+        both = jnp.concatenate(normed[n * heads : (n + 1) * heads], axis=1)
+        tile = (both * gate).astype(jnp.bfloat16)
+        for t in range(ntp):
+            tiles[chip, t] = tile[t * share : (t + 1) * share]
+        k = (farthest + [0])[n]
         for j in range(ntp):
-            source = tiles.at[z_at(k), tp_at(j)]
+            source = tiles.at[chip, tp_at(j)]
             if k or j:
-                copy = remote(
-                    source, out.at[:, place], cs.at[k, j], cr.at[k, j], (dp_at(k), tp_at(j))
+                finals.append(
+                    remote(
+                        source, out.at[:, place], cs.at[k, j], cr.at[k, j], (dp_at(k), tp_at(j))
+                    )
                 )
             else:
                 copy = pltpu.make_async_copy(source, out.at[:, place], cs.at[0, 0])
-            copy.start()
-            finals.append(copy)
+                copy.start()
+                finals.append(copy)
+    for copy in [tok_far] + tok_near + tok_pass + seg_z + tok_y + ba_z + [ba_own]:
+        copy.wait_send()
+    for copy in list(weight_z.values()) + own_sibling + relays:
+        copy.wait_send()
     for copy in finals:
         copy.wait()
 
@@ -515,26 +612,33 @@
     share, model = tokens.shape
     depth = w_query.shape[0]
     value_heads = w_value.shape[1] // DV
-    if n_dp % CORES or w_query.shape[1] // DK != nz or value_heads % nz or rows != 128:
+    if n_dp % (2 * CORES) or w_query.shape[1] // DK != nz or value_heads % nz or rows != 128:
         return shards(*args)
     heads = value_heads // nz
-    wide = 2 * DK + 2 * heads * DV
-    w_ba = jnp.concatenate([w_beta, w_decay], axis=1).T
-    small = w_ba.shape[0]
-    vmem = pl.BlockSpec(memory_space=pltpu.VMEM)
-    anywhere = pl.BlockSpec(memory_space=pl.ANY)
+    small = 2 * value_heads
+    hbm = pl.BlockSpec(memory_space=pltpu.HBM)
     dma = pltpu.SemaphoreType.DMA
+    one_row = norm_gain.reshape(1, -1), decay_rate.reshape(1, -1), dt_bias.reshape(1, -1)
+    gain = out_gain.reshape(1, -1)
+    held = (tokens, one_row[0], w_beta, w_decay, conv_query, conv_key, conv_value)
+    held += one_row[1:] + (gain,)
     return pl.pallas_call(
         functools.partial(layer_kernel, nz, n_tp, heads),
         out_shape=jax.ShapeDtypeStruct((share, n_tp * value_heads * DV), jnp.bfloat16),
-        in_specs=[vmem, vmem] + [anywhere] * 4 + [vmem] * 8,
-        out_specs=vmem,
-        scratch_shapes=[
+        in_specs=[hbm] * 15,
+        out_specs=pl.BlockSpec(memory_space=pltpu.VMEM),
+        scratch_shapes=[pltpu.VMEM(a.shape, a.dtype) for a in held]
+        + [
             pltpu.VMEM((nz, n_tp, share, model), jnp.bfloat16),
-            pltpu.VMEM((n_dp, depth, wide), jnp.bfloat16),
+            pltpu.VMEM((n_dp, depth, 2 * DK), jnp.bfloat16),
+            pltpu.VMEM((n_dp, depth, heads * DV), jnp.bfloat16),
+            pltpu.VMEM((n_dp, depth, heads * DV), jnp.bfloat16),
             pltpu.VMEM((n_dp, small, depth), jnp.bfloat16),
-            pltpu.VMEM((nz, 8, rows), jnp.int32),
+            pltpu.VMEM((nz, 1, rows), jnp.int32),
             pltpu.VMEM((nz, n_tp, share, heads * DV), jnp.bfloat16),
+            dma((11,)),
+            dma((nz,)),
+            dma((nz,)),
             dma((nz,)),
             dma((nz,)),
             dma((nz, n_tp)),
@@ -543,8 +647,8 @@
             dma((nz, 4)),
             dma((4,)),
             dma((4,)),
-            dma((nz,)),
-            dma((nz,)),
+            dma((3, nz)),
+            dma((3, nz)),
             dma((nz,)),
             dma((nz,)),
             dma((nz,)),
@@ -556,23 +660,24 @@
             dma((4,)),
         ],
         compiler_params=pltpu.CompilerParams(
-            collective_id=0, has_side_effects=True, vmem_limit_bytes=48 * 2**20
+            collective_id=0, has_side_effects=True, vmem_limit_bytes=60 * 2**20
         ),
     )(
         tokens,
-        norm_gain.reshape(1, -1),
+        one_row[0],
         w_query,
         w_key,
         w_value,
         w_gate,
-        w_ba,
+        w_beta,
+        w_decay,
         conv_query,
         conv_key,
         conv_value,
-        decay_rate.reshape(1, -1),
-        dt_bias.reshape(1, -1),
-        out_gain.reshape(1, -1),
-        jnp.broadcast_to(seg_ids, (8, rows)),
+        one_row[1],
+        one_row[2],
+        gain,
+        seg_ids,
     )
 
 

time: 82.4 us -> 62.1 us (0.75)
  Pallas kernels: 73.5 us -> 58.1 us
  local copies, waits for them, and re-layouts: 7.67 us -> 3.83 us
    pallas_call x1, Pallas kernels: 73.5 us -> 58.1 us  [layer(): pl.pallas_call(functools.partial(layer_kernel, nz, n_tp, heads), out_shap...]
    unnamed x25 -> x7, local copies, waits for them, and re-layouts: 7 us -> 3.83 us
where the time goes in v2:
time: 62.1 us; the launch traced here: 61.9 us
  Pallas kernels  58.1 us (94%)
  local copies, waits for them, and re-layouts  3.83 us (6%)
    pallas_call x1, Pallas kernels, layer(): pl.pallas_call(functools.partial(layer_kernel, nz, n_tp, heads), out_shap...  58.1 us
    unnamed x7, local copies, waits for them, and re-layouts  3.83 us

profile of v2, /device:TPU:0, one launch (start us, length us, event | category | flops | bytes accessed | tf_op | source)
XLA Modules:
  0.0 61.9 jit_solution(1893165066541206720)
XLA Ops:
  0.0 0.0 copy-start
  0.0 0.7 %copy-done = bf16[256,8]{0,1:T(8,128)(2,1)S(1)} copy-done((bf16[256,8]{0,1:T(8,128)(2,1)S(1)}, bf16[256,8]{0,1:T(8,128)(2,1)}, u32[]{:S(2)}) %copy-start) | copy-done | bytes 4120
  0.7 0.0 copy-start.1
  0.7 0.7 %copy.16.beta_hbm = bf16[256,8]{1,0:T(8,128)(2,1)} copy(bf16[256,8]{0,1:T(8,128)(2,1)S(1)} %copy-done) | data formatting | bytes 8192 | tf_op args[6]
  1.4 0.0 copy-done.1
  1.4 0.7 %copy.17.decay_hbm = bf16[256,8]{1,0:T(8,128)(2,1)} copy(bf16[256,8]{0,1:T(8,128)(2,1)S(1)} %copy-done.1) | data formatting | bytes 8192 | tf_op args[7]
  2.2 58.1 %shard_map.145 = bf16[32,4096]{1,0:T(8,128)(2,1)} custom-call(bf16[32,2048]{1,0:T(8,128)(2,1)} %tokens_hbm.1, f32[1,2048]{1,0:T(1,128)} %bitcast.4, bf16[256,512]{1,0:T(8,128)(2,1)} %w_query.1, bf16[256,512]{1,0:T(8,128)(2,1)} %w_key.1, bf16[256,1024]{1,0:T(8,128)(2,1)} %w_value.1, bf16[256,1024]{1,0:T(8,128)(2,1)} %w_gate.1, bf16[256,8]{1,0:T(8,128)(2,1)} %copy.16.beta_hbm, ...), custom_call_target="tpu_custom_call" | custom-call | tf_op jit(solution)/shard_map/pallas_call | solution.py:625
  60.2 1.7 %copy.19 = bf16[32,4096]{1,0:T(8,128)(2,1)} copy(bf16[32,4096]{1,0:T(8,128)(2,1)} %shard_map.145) | data formatting | bytes 524288
Async XLA Ops:
  0.0 0.7 %copy-start = (bf16[256,8]{0,1:T(8,128)(2,1)S(1)}, bf16[256,8]{0,1:T(8,128)(2,1)}, u32[]{:S(2)}) copy-start(bf16[256,8]{0,1:T(8,128)(2,1)} %param.21) | copy-start | bytes 12292
  0.7 0.7 %copy-start.1 = (bf16[256,8]{0,1:T(8,128)(2,1)S(1)}, bf16[256,8]{0,1:T(8,128)(2,1)}, u32[]{:S(2)}) copy-start(bf16[256,8]{0,1:T(8,128)(2,1)} %param.22) | copy-start | bytes 12292

commit v3 on v2

--- a/solution.py
+++ b/solution.py
@@ -192,6 +192,30 @@
     )
 
 
+def two_parts(values):
+    high = values.astype(jnp.bfloat16)
+    low = (values - high.astype(jnp.float32)).astype(jnp.bfloat16)
+    return high, low
+
+
+def product(left, right):
+    left_parts = jnp.concatenate(two_parts(left), axis=1)
+    right_parts = jnp.concatenate(two_parts(right), axis=1)
+    right_parts = jnp.concatenate([right_parts, right_parts], axis=0)
+    both = jnp.dot(left_parts, right_parts, preferred_element_type=jnp.float32)
+    size = right.shape[1]
+    return both[:, :size] + both[:, size:]
+
+
+def product_rows(left, right):
+    left_parts = jnp.concatenate(two_parts(left), axis=1)
+    right_parts = jnp.concatenate(two_parts(right), axis=0)
+    right_parts = jnp.concatenate([right_parts, right_parts], axis=1)
+    both = dot_rows(left_parts, right_parts)
+    size = right.shape[0]
+    return both[:, :size] + both[:, size:]
+
+
 def sigmoid(x):
     return 1.0 / (1.0 + jnp.exp(-x))
 
@@ -218,15 +242,15 @@
         return row // size == col // size
 
     inner = [jnp.where(block(STEP), m, 0.0) for m in lows]
-    squares = [dot_exact(m, m) for m in inner]
-    fourths = [dot_exact(m, m) for m in squares]
-    firsts = [eye - m + s - dot_exact(m, s) for m, s in zip(inner, squares)]
-    inverse = [f + dot_exact(f, q) for f, q in zip(firsts, fourths)]
+    squares = [product(m, m) for m in inner]
+    fourths = [product(m, m) for m in squares]
+    firsts = [eye - m + s - product(m, s) for m, s in zip(inner, squares)]
+    inverse = [f + product(f, q) for f, q in zip(firsts, fourths)]
     size = STEP
     while size < rows // 4:
         ring = block(2 * size) & jnp.logical_not(block(size))
-        parts = [dot_exact(jnp.where(ring, m, 0.0), t) for m, t in zip(lows, inverse)]
-        inverse = [t - dot_exact(t, p) for t, p in zip(inverse, parts)]
+        parts = [product(jnp.where(ring, m, 0.0), t) for m, t in zip(lows, inverse)]
+        inverse = [t - product(t, p) for t, p in zip(inverse, parts)]
         size = 2 * size
     outer = jnp.logical_not(block(size))
     return inverse, [jnp.where(outer, m, 0.0) for m in lows]
@@ -272,8 +296,6 @@
     loads,
     zs,
     zr,
-    fs,
-    fr,
     ys,
     yr,
     ws,
@@ -302,9 +324,6 @@
     def z_at(k):
         return lax.rem(z + k, nz)
 
-    def z_from(k):
-        return lax.rem(z + nz - k, nz)
-
     def dp_at(k):
         return z_at(k) * CORES + core
 
@@ -333,7 +352,7 @@
         load(1, gain_hbm, norm_gain),
         load(2, beta_hbm, w_beta),
         load(3, decay_hbm, w_decay),
-        load(4, seg_hbm, seg.at[z]),
+        load(4, seg_hbm, seg.at[0]),
     ]
     later = [
         load(5, taps_q_hbm, taps_q),
@@ -361,7 +380,8 @@
             (w_query.at[:, columns(chip, DK)], w_first.at[dp, :, 0:DK]),
             (w_key.at[:, columns(chip, DK)], w_first.at[dp, :, DK : 2 * DK]),
             (w_value.at[:, columns(chip, width)], w_second.at[dp]),
-            (w_gate.at[:, columns(chip, width)], w_third.at[dp]),
+        ) + tuple(
+            (w_gate.at[:, columns(chip * heads + h, DV)], w_third.at[h, dp]) for h in range(heads)
         )
 
     for copy in early:
@@ -374,98 +394,87 @@
 
     floats = tokens[...].astype(jnp.float32)
     scaled = floats * lax.rsqrt(jnp.mean(floats * floats, axis=-1, keepdims=True) + 1e-06)
-    tok[z, tp] = (scaled * norm_gain[...]).astype(jnp.bfloat16)
-    count = w_beta.shape[1]
-    pick_row = lax.broadcasted_iota(jnp.int32, (2 * count, count), 0)
-    pick_col = lax.broadcasted_iota(jnp.int32, (2 * count, count), 1)
-    pick_beta = jnp.where(pick_row == pick_col, 1.0, 0.0).astype(jnp.bfloat16)
-    pick_decay = jnp.where(pick_row == pick_col + count, 1.0, 0.0).astype(jnp.bfloat16)
-    ba[dp] = (dot_rows(pick_beta, w_beta[...]) + dot_rows(pick_decay, w_decay[...])).astype(
-        jnp.bfloat16
-    )
+    tok[0, tp] = (scaled * norm_gain[...]).astype(jnp.bfloat16)
+    count = w_beta.shape[0]
+    narrow = [w_beta[...].astype(jnp.float32), w_decay[...].astype(jnp.float32)]
+    ba[dp] = jnp.concatenate(narrow, axis=0).astype(jnp.bfloat16)
 
     pl.semaphore_wait(barrier, nz * ntp)
 
     half = nz // 2
-    near = [k for k in range(1, half)]
-    far = half
-    mirror = z + half - 2 * half * (z // half)
-
-    def in_half(k):
-        return (z // half) * half + lax.rem(z + k, half)
-
-    def in_half_from(k):
-        return (z // half) * half + lax.rem(z + half - k, half)
-
-    def other(chip):
-        return lax.rem(chip + half, nz)
+    base = (z // half) * half
+    mirror = lax.rem(z + half, nz)
+    targets = [z, mirror]
+    sources = [z, mirror]
+    for k in range(1, half):
+        ahead = base + lax.rem(z + k, half)
+        behind = base + lax.rem(z + half - k, half)
+        targets += [ahead, lax.rem(ahead + half, nz)]
+        sources += [behind, lax.rem(behind + half, nz)]
+    others = range(1, nz)
+    evens = range(2, nz, 2)
 
     def device_of(chip):
         return (chip * CORES + core, tp)
 
-    tok_far = remote(
-        tok.at[z, tp], tok.at[z, tp], zs.at[far], zr.at[far], device_of(mirror)
-    )
-    tok_near = [
-        remote(tok.at[z, tp], tok.at[z, tp], zs.at[k], zr.at[k], device_of(in_half(k)))
-        for k in near
-    ]
+    def send_rows(source, slot):
+        return remote(
+            tok.at[source, tp],
+            tok.at[slot, tp],
+            zs.at[slot],
+            zr.at[slot],
+            device_of(targets[slot - source]),
+        )
+
+    def spread_rows(slot):
+        return [
+            remote(
+                tok.at[slot, tp], tok.at[slot, tp], ys.at[slot, j], yr.at[slot, j], (dp, tp_at(j))
+            )
+            for j in range(1, ntp)
+        ]
+
+    tok_z = {1: send_rows(0, 1)}
+    for n in evens:
+        tok_z[n] = send_rows(0, n)
+    tok_y = {0: spread_rows(0)}
     seg_z = []
     ba_z = []
-    for k in range(1, nz):
-        peer = (dp_at(k), tp)
-        seg_z.append(remote(seg.at[z], seg.at[z], ss.at[k], sr.at[k], peer))
-        ba_z.append(remote(ba.at[dp], ba.at[dp], bs.at[k], br.at[k], peer))
-
-    def spread_rows(n, at):
-        return [
-            remote(tok.at[at, tp], tok.at[at, tp], ys.at[n, j], yr.at[n, j], (dp, tp_at(j)))
-            for j in range(1, ntp)
-        ]
-
-    tok_y = spread_rows(0, z)
-    farthest = [nz // 2] + [k for k in range(1, nz) if k != nz // 2]
+    for n in others:
+        peer = device_of(targets[n])
+        seg_z.append(remote(seg.at[0], seg.at[n], ss.at[n], sr.at[n], peer))
+        ba_z.append(remote(ba.at[dp], ba.at[dp], bs.at[n], br.at[n], peer))
+
     weight_z = {}
-    for i in range(4):
-        for k in farthest:
-            source, target = pieces(z_at(k))[i]
-            weight_z[i, k] = remote(source, target, ws.at[k, i], wr.at[k, i], (dp_at(k), tp))
+    for i in range(3 + heads):
+        for n in others:
+            source, target = pieces(targets[n])[i]
+            weight_z[i, n] = remote(
+                source, target, ws.at[n, i], wr.at[n, i], device_of(targets[n])
+            )
         if i == 1:
-            tok_far.wait_recv()
-            tok_pass = [
-                remote(
-                    tok.at[mirror, tp],
-                    tok.at[mirror, tp],
-                    fs.at[k],
-                    fr.at[k],
-                    device_of(in_half(k)),
-                )
-                for k in near
-            ]
-            tok_y += spread_rows(1, mirror)
+            tok_z[1].wait_recv()
+            for n in evens:
+                tok_z[n + 1] = send_rows(1, n + 1)
+            tok_y[1] = spread_rows(1)
     own_sibling = []
     for i, (source, target) in enumerate(pieces(z)):
         own_sibling.append(remote(source, target, os.at[i], orr.at[i], sibling))
     ba_own = remote(ba.at[dp], ba.at[dp], brs.at[0], brr.at[0], sibling)
-
-    slot = 2
-    for k in near:
-        tok_near[k - 1].wait_recv()
-        tok_y += spread_rows(slot, in_half_from(k))
-        tok_pass[k - 1].wait_recv()
-        tok_y += spread_rows(slot + 1, other(in_half_from(k)))
-        slot += 2
+    for n in range(2, nz):
+        tok_z[n].wait_recv()
+        tok_y[n] = spread_rows(n)
 
     relays = []
 
     def relay(stage, which, ref):
         passed = []
-        for k in farthest:
-            at = z_from(k) * CORES + core
+        for n in others:
+            at = sources[n] * CORES + core
             for i in which:
-                weight_z[i, k].wait_recv()
+                weight_z[i, n].wait_recv()
             passed.append(
-                remote(ref.at[at], ref.at[at], rs.at[stage, k], rr.at[stage, k], sibling)
+                remote(ref.at[at], ref.at[at], rs.at[stage, n], rr.at[stage, n], sibling)
             )
         for i in which:
             own_local[i].wait()
@@ -474,21 +483,18 @@
             copy.wait_recv()
         relays.extend(passed)
 
-    for k in range(1, nz):
-        at = z_from(k) * CORES + core
-        ba_z[k - 1].wait_recv()
-        relays.append(remote(ba.at[at], ba.at[at], brs.at[k], brr.at[k], sibling))
-    ba_own.wait_recv()
-    for copy in list(relays):
-        copy.wait_recv()
-    for copy in seg_z + tok_y:
-        copy.wait_recv()
+    for n in others:
+        at = sources[n] * CORES + core
+        ba_z[n - 1].wait_recv()
+        relays.append(remote(ba.at[at], ba.at[at], brs.at[n], brr.at[n], sibling))
     for copy in later:
         copy.wait()
+    for copy in [ba_own] + relays + seg_z:
+        copy.wait_recv()
     relay(0, (0, 1), w_first)
 
     rows = seg.shape[2]
-    sources, depth = ba.shape[0], ba.shape[2]
+    holders, depth = ba.shape[0], ba.shape[2]
     model = tok.shape[3]
     row = lax.broadcasted_iota(jnp.int32, (rows, rows), 0)
     col = lax.broadcasted_iota(jnp.int32, (rows, rows), 1)
@@ -497,91 +503,98 @@
     ones_lower = jnp.where(lower, 1.0, 0.0)
     lane = lax.broadcasted_iota(jnp.int32, (rows, count), 1)
 
-    def project(chip, ref):
-        left = tok[chip].reshape(rows, model)
-        right = ref[...].reshape(sources * depth, ref.shape[2])
+    def project(first, slots, ref):
+        left = tok[first : first + slots].reshape(slots * rows, model)
+        right = ref[...].reshape(holders * depth, ref.shape[-1])
         result = jnp.dot(left, right, preferred_element_type=jnp.float32)
         return result.astype(jnp.bfloat16).astype(jnp.float32)
 
-    order = [z_at(k) for k in farthest] + [z]
     tq = taps_q[:, columns(z, DK)]
     tk = taps_k[:, columns(z, DK)]
     tv = taps_v[:, columns(z, width)]
-    lows, scores, betas, befores = [], [], [], []
-    for chip in order:
-        projected = project(chip, w_first)
-        left = tok[chip].reshape(rows, model)
-        small = jnp.zeros((rows, 2 * count), jnp.float32)
-        for s in range(sources):
+    inverse, outer, scores, betas, befores = [], [], [], [], []
+    for first in range(0, nz, 2):
+        for n in (first, first + 1):
+            for copy in tok_y[n]:
+                copy.wait_recv()
+        pair = project(first, 2, w_first)
+        left = tok[first : first + 2].reshape(2 * rows, model)
+        small = jnp.zeros((2 * rows, 2 * count), jnp.float32)
+        for s in range(holders):
             small = small + dot_rows(left[:, s * depth : (s + 1) * depth], ba[s])
         small = small.astype(jnp.bfloat16).astype(jnp.float32)
-        beta_all = sigmoid(small[:, :count])
-        shifted = small[:, count:] + bias[...]
-        soft = jnp.maximum(shifted, 0.0) + jnp.log1p(jnp.exp(-jnp.abs(shifted)))
-        cumulative = dot_exact(ones_lower, -rate[...] * soft)
-        seg_row = jnp.broadcast_to(seg[chip].astype(jnp.float32), (rows, rows))
-        seg_col = seg_row.T
-        same = seg_row == seg_col
-        same_before = [
-            (pltpu.roll(seg_col, offset, 0) == seg_col) & (row >= offset) for offset in range(1, 4)
-        ]
-        query = unit_rows(conv_rows(projected[:, :DK], tq, same_before)) * DK ** (-0.5)
-        key = unit_rows(conv_rows(projected[:, DK:], tk, same_before))
-        key_gram = dot_rows(key, key, highest)
-        query_gram = dot_rows(query, key, highest)
-        befores.append(same_before)
-        for h in range(heads):
-            pick = lane == z * heads + h
-            beta = jnp.sum(jnp.where(pick, beta_all, 0.0), axis=1, keepdims=True)
-            total = jnp.sum(jnp.where(pick, cumulative, 0.0), axis=1, keepdims=True)
-            total = jnp.broadcast_to(total, (rows, rows))
-            spread = jnp.where(lower, total - total.T, 0.0)
-            decay = jnp.where(lower & same, jnp.exp(spread), 0.0)
-            betas.append(beta)
-            lows.append(jnp.where(strict, beta * key_gram * decay, 0.0))
-            scores.append(query_gram * decay)
-    inverse, outer = inverse_blocks(lows, row, col, rows)
+        lows = []
+        for n in (first, first + 1):
+            at = (n - first) * rows
+            projected = pair[at : at + rows]
+            beta_all = sigmoid(small[at : at + rows, :count])
+            shifted = small[at : at + rows, count:] + bias[...]
+            soft = jnp.maximum(shifted, 0.0) + jnp.log1p(jnp.exp(-jnp.abs(shifted)))
+            cumulative = dot_exact(ones_lower, -rate[...] * soft)
+            seg_row = jnp.broadcast_to(seg[n].astype(jnp.float32), (rows, rows))
+            seg_col = seg_row.T
+            same = seg_row == seg_col
+            same_before = [
+                (pltpu.roll(seg_col, offset, 0) == seg_col) & (row >= offset)
+                for offset in range(1, 4)
+            ]
+            query = unit_rows(conv_rows(projected[:, :DK], tq, same_before)) * DK ** (-0.5)
+            key = unit_rows(conv_rows(projected[:, DK:], tk, same_before))
+            key_gram = product_rows(key, key)
+            query_gram = product_rows(query, key)
+            befores.append(same_before)
+            for h in range(heads):
+                pick = lane == z * heads + h
+                beta = jnp.sum(jnp.where(pick, beta_all, 0.0), axis=1, keepdims=True)
+                total = jnp.sum(jnp.where(pick, cumulative, 0.0), axis=1, keepdims=True)
+                total = jnp.broadcast_to(total, (rows, rows))
+                spread = jnp.where(lower, total - total.T, 0.0)
+                decay = jnp.where(lower & same, jnp.exp(spread), 0.0)
+                betas.append(beta)
+                lows.append(jnp.where(strict, beta * key_gram * decay, 0.0))
+                scores.append(query_gram * decay)
+        blocks, rest = inverse_blocks(lows, row, col, rows)
+        inverse += blocks
+        outer += rest
 
     relay(1, (2,), w_second)
     rights = []
-    for n, chip in enumerate(order):
-        values = conv_rows(project(chip, w_second), tv, befores[n])
+    projected = project(0, nz, w_second)
+    for n in range(nz):
+        values = conv_rows(projected[n * rows : (n + 1) * rows], tv, befores[n])
         for h in range(heads):
             rights.append(betas[n * heads + h] * values[:, h * DV : (h + 1) * DV])
-    solved = [dot_exact(t, b) for t, b in zip(inverse, rights)]
-    parts = [dot_exact(m, x) for m, x in zip(outer, solved)]
-    solved = [x - dot_exact(t, p) for x, t, p in zip(solved, inverse, parts)]
-    mixed = [dot_exact(s, x) for s, x in zip(scores, solved)]
+    solved = [product(t, b) for t, b in zip(inverse, rights)]
+    parts = [product(m, x) for m, x in zip(outer, solved)]
+    solved = [x - product(t, p) for x, t, p in zip(solved, inverse, parts)]
+    mixed = [product(s, x) for s, x in zip(scores, solved)]
     normed = [
         m * lax.rsqrt(jnp.mean(m * m, axis=-1, keepdims=True) + 1e-06) * out_gain[...]
         for m in mixed
     ]
 
-    relay(2, (3,), w_third)
-    place = columns(tp * nz + z, width)
     share = rows // ntp
     finals = []
-    for n, chip in enumerate(order):
-        gate = project(chip, w_third)
-        gate = gate * sigmoid(gate)
-        both = jnp.concatenate(normed[n * heads : (n + 1) * heads], axis=1)
-        tile = (both * gate).astype(jnp.bfloat16)
-        for t in range(ntp):
-            tiles[chip, t] = tile[t * share : (t + 1) * share]
-        k = (farthest + [0])[n]
-        for j in range(ntp):
-            source = tiles.at[chip, tp_at(j)]
-            if k or j:
-                finals.append(
-                    remote(
-                        source, out.at[:, place], cs.at[k, j], cr.at[k, j], (dp_at(k), tp_at(j))
-                    )
-                )
-            else:
-                copy = pltpu.make_async_copy(source, out.at[:, place], cs.at[0, 0])
-                copy.start()
-                finals.append(copy)
-    for copy in [tok_far] + tok_near + tok_pass + seg_z + tok_y + ba_z + [ba_own]:
+    for h in range(heads):
+        relay(2 + h, (3 + h,), w_third.at[h])
+        place = columns((tp * nz + z) * heads + h, DV)
+        gates = project(0, nz, w_third.at[h])
+        for n in list(others) + [0]:
+            gate = gates[n * rows : (n + 1) * rows]
+            tile = (normed[n * heads + h] * (gate * sigmoid(gate))).astype(jnp.bfloat16)
+            for t in range(ntp):
+                tiles[h, n, t] = tile[t * share : (t + 1) * share]
+            for j in range(ntp):
+                source = tiles.at[h, n, tp_at(j)]
+                target = out.at[:, place]
+                if n or j:
+                    device = (sources[n] * CORES + core, tp_at(j))
+                    finals.append(remote(source, target, cs.at[h, n, j], cr.at[h, n, j], device))
+                else:
+                    copy = pltpu.make_async_copy(source, target, cs.at[h, 0, 0])
+                    copy.start()
+                    finals.append(copy)
+    for copy in list(tok_z.values()) + sum(tok_y.values(), []) + seg_z + ba_z + [ba_own]:
         copy.wait_send()
     for copy in list(weight_z.values()) + own_sibling + relays:
         copy.wait_send()
@@ -620,44 +633,43 @@
     dma = pltpu.SemaphoreType.DMA
     one_row = norm_gain.reshape(1, -1), decay_rate.reshape(1, -1), dt_bias.reshape(1, -1)
     gain = out_gain.reshape(1, -1)
-    held = (tokens, one_row[0], w_beta, w_decay, conv_query, conv_key, conv_value)
+    narrow = w_beta.T, w_decay.T
+    held = (tokens, one_row[0], *narrow, conv_query, conv_key, conv_value)
     held += one_row[1:] + (gain,)
     return pl.pallas_call(
         functools.partial(layer_kernel, nz, n_tp, heads),
         out_shape=jax.ShapeDtypeStruct((share, n_tp * value_heads * DV), jnp.bfloat16),
         in_specs=[hbm] * 15,
-        out_specs=pl.BlockSpec(memory_space=pltpu.VMEM),
+        out_specs=hbm,
         scratch_shapes=[pltpu.VMEM(a.shape, a.dtype) for a in held]
         + [
             pltpu.VMEM((nz, n_tp, share, model), jnp.bfloat16),
             pltpu.VMEM((n_dp, depth, 2 * DK), jnp.bfloat16),
             pltpu.VMEM((n_dp, depth, heads * DV), jnp.bfloat16),
-            pltpu.VMEM((n_dp, depth, heads * DV), jnp.bfloat16),
+            pltpu.VMEM((heads, n_dp, depth, DV), jnp.bfloat16),
             pltpu.VMEM((n_dp, small, depth), jnp.bfloat16),
             pltpu.VMEM((nz, 1, rows), jnp.int32),
-            pltpu.VMEM((nz, n_tp, share, heads * DV), jnp.bfloat16),
+            pltpu.VMEM((heads, nz, n_tp, share, DV), jnp.bfloat16),
             dma((11,)),
-            dma((nz,)),
-            dma((nz,)),
             dma((nz,)),
             dma((nz,)),
             dma((nz, n_tp)),
             dma((nz, n_tp)),
-            dma((nz, 4)),
-            dma((nz, 4)),
-            dma((4,)),
-            dma((4,)),
-            dma((3, nz)),
-            dma((3, nz)),
+            dma((nz, 3 + heads)),
+            dma((nz, 3 + heads)),
+            dma((3 + heads,)),
+            dma((3 + heads,)),
+            dma((2 + heads, nz)),
+            dma((2 + heads, nz)),
             dma((nz,)),
             dma((nz,)),
             dma((nz,)),
             dma((nz,)),
             dma((nz,)),
             dma((nz,)),
-            dma((nz, n_tp)),
-            dma((nz, n_tp)),
-            dma((4,)),
+            dma((heads, nz, n_tp)),
+            dma((heads, nz, n_tp)),
+            dma((3 + heads,)),
         ],
         compiler_params=pltpu.CompilerParams(
             collective_id=0, has_side_effects=True, vmem_limit_bytes=60 * 2**20
@@ -669,8 +681,7 @@
         w_key,
         w_value,
         w_gate,
-        w_beta,
-        w_decay,
+        *narrow,
         conv_query,
         conv_key,
         conv_value,

time: 62.1 us -> 59.3 us (0.955)
  local copies, waits for them, and re-layouts: 3.83 us -> 1.67 us
  Pallas kernels: 58.1 us -> 57.4 us
    unnamed x7 -> x1, local copies, waits for them, and re-layouts: 3.83 us -> 1.67 us
    pallas_call x1, Pallas kernels: 58.1 us -> 57.4 us  [layer(): pl.pallas_call(functools.partial(layer_kernel, nz, n_tp, heads), out_shap...]
where the time goes in v3:
time: 59.3 us; the launch traced here: 59.1 us
  Pallas kernels  57.4 us (97%)
  local copies, waits for them, and re-layouts  1.67 us (3%)
    pallas_call x1, Pallas kernels, layer(): pl.pallas_call(functools.partial(layer_kernel, nz, n_tp, heads), out_shap...  57.4 us
    unnamed x1, local copies, waits for them, and re-layouts  1.67 us

profile of v3, /device:TPU:0, one launch (start us, length us, event | category | flops | bytes accessed | tf_op | source)
XLA Modules:
  0.0 59.1 jit_solution(17734790765157112086)
XLA Ops:
  0.0 57.4 %shard_map.145 = bf16[32,4096]{1,0:T(8,128)(2,1)} custom-call(bf16[32,2048]{1,0:T(8,128)(2,1)} %tokens_hbm.1, f32[1,2048]{1,0:T(1,128)} %bitcast.6, bf16[256,512]{1,0:T(8,128)(2,1)} %w_query.1, bf16[256,512]{1,0:T(8,128)(2,1)} %w_key.1, bf16[256,1024]{1,0:T(8,128)(2,1)} %w_value.1, bf16[256,1024]{1,0:T(8,128)(2,1)} %w_gate.1, bf16[8,256]{1,0:T(8,128)(2,1)} %bitcast.7, ...), custom_call_target="tpu_custom_call" | custom-call | tf_op jit(solution)/shard_map/pallas_call | solution.py:639
  57.4 1.7 %copy.17 = bf16[32,4096]{1,0:T(8,128)(2,1)} copy(bf16[32,4096]{1,0:T(8,128)(2,1)} %shard_map.145) | data formatting | bytes 524288

commit v4 on v3

--- a/solution.py
+++ b/solution.py
@@ -413,6 +413,7 @@
         sources += [behind, lax.rem(behind + half, nz)]
     others = range(1, nz)
     evens = range(2, nz, 2)
+    crossing = list(range(1, nz, 2)) + list(evens)
 
     def device_of(chip):
         return (chip * CORES + core, tp)
@@ -446,17 +447,20 @@
         ba_z.append(remote(ba.at[dp], ba.at[dp], bs.at[n], br.at[n], peer))
 
     weight_z = {}
-    for i in range(3 + heads):
-        for n in others:
+
+    def send_weights(i):
+        for n in crossing:
             source, target = pieces(targets[n])[i]
             weight_z[i, n] = remote(
                 source, target, ws.at[n, i], wr.at[n, i], device_of(targets[n])
             )
-        if i == 1:
-            tok_z[1].wait_recv()
-            for n in evens:
-                tok_z[n + 1] = send_rows(1, n + 1)
-            tok_y[1] = spread_rows(1)
+
+    send_weights(0)
+    send_weights(1)
+    tok_z[1].wait_recv()
+    for n in evens:
+        tok_z[n + 1] = send_rows(1, n + 1)
+    tok_y[1] = spread_rows(1)
     own_sibling = []
     for i, (source, target) in enumerate(pieces(z)):
         own_sibling.append(remote(source, target, os.at[i], orr.at[i], sibling))
@@ -464,18 +468,22 @@
     for n in range(2, nz):
         tok_z[n].wait_recv()
         tok_y[n] = spread_rows(n)
+    send_weights(2)
 
     relays = []
 
     def relay(stage, which, ref):
         passed = []
-        for n in others:
+        for n in crossing:
             at = sources[n] * CORES + core
             for i in which:
                 weight_z[i, n].wait_recv()
             passed.append(
                 remote(ref.at[at], ref.at[at], rs.at[stage, n], rr.at[stage, n], sibling)
             )
+        ahead = which[-1] + 2
+        if ahead < 3 + heads:
+            send_weights(ahead)
         for i in which:
             own_local[i].wait()
             own_sibling[i].wait_recv()
@@ -579,7 +587,7 @@
         relay(2 + h, (3 + h,), w_third.at[h])
         place = columns((tp * nz + z) * heads + h, DV)
         gates = project(0, nz, w_third.at[h])
-        for n in list(others) + [0]:
+        for n in crossing + [0]:
             gate = gates[n * rows : (n + 1) * rows]
             tile = (normed[n * heads + h] * (gate * sigmoid(gate))).astype(jnp.bfloat16)
             for t in range(ntp):

time: 59.3 us -> 60.6 us (1.022)
  Pallas kernels: 57.4 us -> 58.7 us
    pallas_call x1, Pallas kernels: 57.4 us -> 58.7 us  [layer(): pl.pallas_call(functools.partial(layer_kernel, nz, n_tp, heads), out_shap...]
where the time goes in v4:
time: 60.6 us; the launch traced here: 60.4 us
  Pallas kernels  58.7 us (97%)
  local copies, waits for them, and re-layouts  1.67 us (3%)
    pallas_call x1, Pallas kernels, layer(): pl.pallas_call(functools.partial(layer_kernel, nz, n_tp, heads), out_shap...  58.7 us
    unnamed x1, local copies, waits for them, and re-layouts  1.67 us

profile of v4, /device:TPU:0, one launch (start us, length us, event | category | flops | bytes accessed | tf_op | source)
XLA Modules:
  0.0 60.4 jit_solution(14628969535572724757)
XLA Ops:
  0.0 58.7 %shard_map.145 = bf16[32,4096]{1,0:T(8,128)(2,1)} custom-call(bf16[32,2048]{1,0:T(8,128)(2,1)} %tokens_hbm.1, f32[1,2048]{1,0:T(1,128)} %bitcast.6, bf16[256,512]{1,0:T(8,128)(2,1)} %w_query.1, bf16[256,512]{1,0:T(8,128)(2,1)} %w_key.1, bf16[256,1024]{1,0:T(8,128)(2,1)} %w_value.1, bf16[256,1024]{1,0:T(8,128)(2,1)} %w_gate.1, bf16[8,256]{1,0:T(8,128)(2,1)} %bitcast.7, ...), custom_call_target="tpu_custom_call" | custom-call | tf_op jit(solution)/shard_map/pallas_call | solution.py:647
  58.7 1.7 %copy.17 = bf16[32,4096]{1,0:T(8,128)(2,1)} copy(bf16[32,4096]{1,0:T(8,128)(2,1)} %shard_map.145) | data formatting | bytes 524288

commit v5 on v4

--- a/solution.py
+++ b/solution.py
@@ -468,7 +468,8 @@
     for n in range(2, nz):
         tok_z[n].wait_recv()
         tok_y[n] = spread_rows(n)
-    send_weights(2)
+    for i in range(2, 3 + heads):
+        send_weights(i)
 
     relays = []
 
@@ -481,9 +482,6 @@
             passed.append(
                 remote(ref.at[at], ref.at[at], rs.at[stage, n], rr.at[stage, n], sibling)
             )
-        ahead = which[-1] + 2
-        if ahead < 3 + heads:
-            send_weights(ahead)
         for i in which:
             own_local[i].wait()
             own_sibling[i].wait_recv()

time: 60.6 us -> 60.5 us (level)
  no operation moved by 1% of the time
where the time goes in v5:
time: 60.5 us; the launch traced here: 60.4 us
  Pallas kernels  58.7 us (97%)
  local copies, waits for them, and re-layouts  1.67 us (3%)
    pallas_call x1, Pallas kernels, layer(): pl.pallas_call(functools.partial(layer_kernel, nz, n_tp, heads), out_shap...  58.7 us
    unnamed x1, local copies, waits for them, and re-layouts  1.67 us

profile of v5, /device:TPU:0, one launch (start us, length us, event | category | flops | bytes accessed | tf_op | source)
XLA Modules:
  0.0 60.4 jit_solution(1911589501924396786)
XLA Ops:
  0.0 58.7 %shard_map.145 = bf16[32,4096]{1,0:T(8,128)(2,1)} custom-call(bf16[32,2048]{1,0:T(8,128)(2,1)} %tokens_hbm.1, f32[1,2048]{1,0:T(1,128)} %bitcast.6, bf16[256,512]{1,0:T(8,128)(2,1)} %w_query.1, bf16[256,512]{1,0:T(8,128)(2,1)} %w_key.1, bf16[256,1024]{1,0:T(8,128)(2,1)} %w_value.1, bf16[256,1024]{1,0:T(8,128)(2,1)} %w_gate.1, bf16[8,256]{1,0:T(8,128)(2,1)} %bitcast.7, ...), custom_call_target="tpu_custom_call" | custom-call | tf_op jit(solution)/shard_map/pallas_call | solution.py:645
  58.7 1.7 %copy.17 = bf16[32,4096]{1,0:T(8,128)(2,1)} copy(bf16[32,4096]{1,0:T(8,128)(2,1)} %shard_map.145) | data formatting | bytes 524288
